TPU v7x, 1024 devices: a whole 8x8x8 slice. The times are simulated.
1024 devices in a mesh: tiles: 128 (over x, z, core), sub: 8 (over y).
Axes of the slice: x: 8, y: 8, z: 8, core: 2. Of those that a mesh axis runs over, the one named last changes fastest.
Arguments:
- state: float32 [1024, 4, 2, 3600], P(('tiles', 'sub')), may hold values from -6 to 6
- surface: float32 [1024, 3600], P(('tiles', 'sub')), may hold values from -6 to 6
- land_mask: int32 [1024, 3600], P(('tiles', 'sub')), may hold values 0 or 1
- neighbours: int32 [1024, 4], P(('tiles', 'sub')), may hold values from -1 to 1023, as said below
Outputs:
- new_state: float32 [1024, 4, 2, 3600], P(('tiles', 'sub'))
- new_surface: float32 [1024, 3600], P(('tiles', 'sub'))
Inputs may be any that keep to these rules, and one draw needn't show every extreme that they name: Every listed tile g satisfies g // 8 differing from the tile's own index // 8 by at most 1; tiles are ocean tiles of a grid of 128 columns, each of 8 ocean tiles in some order, and the lists are those of that grid: north and south neighbours lie in the tile's own column, an east neighbour in the next column, a west neighbour in the previous column.
All inputs are finite; a program needn't handle non-finite values. No bound on the sum of `land_mask` on one device may be relied on, other than what follows from the above.
Results may differ from a plain program's by a relative error of at most 0.0001.
Values sent between devices are 32-bit elements; how exact they have to be, the bound alone decides.
A program may use at most 32 MiB of HBM per device.

v0:
```python
import jax
import jax.numpy as jnp
from jax import lax
from jax.sharding import PartitionSpec as P

TILE = 60
STEPS = 2
SUBCYCLES = 4


time_step = 0.2
mixing = 0.02
coriolis = 0.5
gravity_step = 0.25
depth_step = 0.25


def padded_2(array, sides, width):
    for axis, dim in sides:
        count, length = (lax.axis_size(axis), array.shape[dim])
        up = [(i, (i + 1) % count) for i in range(count - 1)]
        down = [(j, i) for i, j in up]
        last = lax.slice_in_dim(array, length - width, length, axis=dim)
        leading = lax.slice_in_dim(array, 0, width, axis=dim)
        before = lax.ppermute(last, axis, up)
        after = lax.ppermute(leading, axis, down)
        array = jnp.concatenate([before, array, after], axis=dim)
    return array


def edge_panels(field):
    north = field[..., 0:2, :]
    south = field[..., ::-1, :][..., 0:2, :]
    west = jnp.swapaxes(field[..., :, 0:2], -1, -2)
    east = jnp.swapaxes(field[..., :, ::-1][..., :, 0:2], -1, -2)
    stacked = jnp.stack([north, east, south, west], axis=-3)
    return stacked.reshape(field.shape[:-2] + (8 * TILE,))


def pick(candidates, index, valid):
    result = []
    for direction in range(4):
        rows = jnp.take(candidates, index[:, direction], axis=0)
        rows = rows.reshape(rows.shape[:-1] + (4, 2, TILE))[..., (direction + 2) % 4, :, :]
        keep = valid[:, direction].reshape((-1,) + (1,) * (rows.ndim - 1))
        result.append(jnp.where(keep, rows, jnp.zeros_like(rows)))
    return result


def extend(field, north, east, south, west):
    corner = jnp.zeros(field.shape[:-2] + (2, 2), field.dtype)
    top = jnp.concatenate([corner, north[..., ::-1, :], corner], -1)
    bottom = jnp.concatenate([corner, south, corner], -1)
    left = jnp.swapaxes(west[..., ::-1, :], -1, -2)
    right = jnp.swapaxes(east, -1, -2)
    middle = jnp.concatenate([left, field, right], -1)
    return jnp.concatenate([top, middle, bottom], -2)


def laplace(field):
    widths = [(0, 0)] * (field.ndim - 2) + [(1, 1), (1, 1)]
    padded = jnp.pad(field, widths)
    return (
        padded[..., 2:, 1:-1]
        + padded[..., :-2, 1:-1]
        + padded[..., 1:-1, 2:]
        + padded[..., 1:-1, :-2]
        - 4.0 * field
    )


def clinic(fields, extended, wet):
    last = TILE + 2
    grad_x = (extended[..., 2:last, 3 : last + 1] - extended[..., 2:last, 1 : last - 1]) * 0.5
    grad_y = (extended[..., 3 : last + 1, 2:last] - extended[..., 1 : last - 1, 2:last]) * 0.5
    smooth = laplace(laplace(extended))[..., 2:last, 2:last]
    zonal = fields[..., 2, :, :, :]
    meridional = fields[..., 3, :, :, :]
    tend = -(zonal * grad_x + meridional * grad_y) - mixing * smooth
    nothing = jnp.zeros_like(zonal)
    turning = jnp.stack([nothing, nothing, coriolis * meridional, -coriolis * zonal], axis=-4)
    return (fields + time_step * (tend + turning)) * wet


def depth_sum(field):
    levels = field.shape[-3]
    weights = 2.0 * (jnp.arange(levels).astype(jnp.float32) + 1.0) / (levels * (levels + 1))
    return jnp.sum(field * weights[:, None, None], axis=-3)


def tropic(height, zonal, meridional, wet):
    full = TILE + 4
    grad_x = (height[..., 1 : full - 1, 2:full] - height[..., 1 : full - 1, 0 : full - 2]) * 0.5
    grad_y = (height[..., 2:full, 1 : full - 1] - height[..., 0 : full - 2, 1 : full - 1]) * 0.5
    new_u = zonal[..., 1 : full - 1, 1 : full - 1] - gravity_step * grad_x
    new_v = meridional[..., 1 : full - 1, 1 : full - 1] - gravity_step * grad_y
    last = TILE + 1
    spread = (
        new_u[..., 1:last, 2 : last + 1]
        - new_u[..., 1:last, 0 : last - 1]
        + new_v[..., 2 : last + 1, 1:last]
        - new_v[..., 0 : last - 1, 1:last]
    ) * 0.5
    height_new = (height[..., 2 : last + 1, 2 : last + 1] - depth_step * spread) * wet
    return (height_new, new_u[..., 1:last, 1:last] * wet, new_v[..., 1:last, 1:last] * wet)


def couple(fields, change_u, change_v):
    zonal = fields[:, 2] + change_u[:, None]
    meridional = fields[:, 3] + change_v[:, None]
    return jnp.concatenate([fields[:, 0:2], zonal[:, None], meridional[:, None]], axis=1)


def clinic_halos(panels, neighbours, valid):
    count = panels.shape[0]
    slots = count * lax.axis_size("sub")
    column = lax.axis_index("tiles")
    group = lax.all_gather(panels, "sub", axis=0, tiled=True)
    candidates = padded_2(group, (("tiles", 0),), slots)
    index = neighbours - (column - 1) * slots
    index = jnp.where(valid, index, 0)
    return pick(candidates, index, valid)


def surface_halos(panels, neighbours, valid):
    count = panels.shape[0]
    slots = count * lax.axis_size("sub")
    column = lax.axis_index("tiles")
    group = lax.all_gather(panels, "sub", axis=0, tiled=True)
    candidates = padded_2(group, (("tiles", 0),), slots)
    index = jnp.where(valid, neighbours - (column - 1) * slots, 0)
    return pick(candidates, index, valid)


def shards(state, surface, land_mask, neighbours):
    count = state.shape[0]
    levels = state.shape[2]
    wet = land_mask.reshape(count, TILE, TILE).astype(jnp.float32)
    fields = state.reshape(count, 4, levels, TILE, TILE) * wet[:, None, None]
    height = surface.reshape(count, TILE, TILE) * wet
    valid = neighbours >= 0
    for step in range(STEPS):
        halos = clinic_halos(edge_panels(fields), neighbours, valid)
        extended = extend(fields, halos[0], halos[1], halos[2], halos[3])
        fields = clinic(fields, extended, wet[:, None, None])
        old_u = depth_sum(fields[:, 2])
        old_v = depth_sum(fields[:, 3])
        zonal, meridional = (old_u, old_v)
        for cycle in range(SUBCYCLES):
            stacked = jnp.stack([height, zonal, meridional], axis=1)
            near = surface_halos(edge_panels(stacked), neighbours, valid)
            widened = extend(stacked, near[0], near[1], near[2], near[3])
            height, zonal, meridional = tropic(widened[:, 0], widened[:, 1], widened[:, 2], wet)
        fields = couple(fields, zonal - old_u, meridional - old_v)
    return (fields.reshape(count, 4, levels, TILE * TILE), height.reshape(count, TILE * TILE))


def solution(mesh):
    in_specs = (
        P(("tiles", "sub"), None, None, None),
        P(("tiles", "sub"), None),
        P(("tiles", "sub"), None),
        P(("tiles", "sub"), None),
    )
    out_specs = (P(("tiles", "sub"), None, None, None), P(("tiles", "sub"), None))
    return jax.shard_map(shards, mesh=mesh, in_specs=in_specs, out_specs=out_specs, check_vma=False)
```

profile of v0, /device:TPU:8, one launch (start us, length us, event | category | flops | bytes accessed | tf_op | source)
XLA Modules:
  0.0 424.1 jit_solution(12215912405830030967)
XLA Ops:
  0.6 0.8 multiply_reduce_fusion
  1.5 1.3 reshape.1065
  4.3 26.9 %all_gather.30 = f32[8,4,2,480]{3,1,2,0:T(4,128)S(1)} all-gather(f32[1,4,2,480]{3,1,2,0:T(4,128)S(1)} %reshape.1557), channel_id=1, replica_groups=mesh['tiles'=128,'sub'=8] {'sub'}, dimensions={0}, use_global_device_ids=true | all-gather | bytes 138240 | tf_op jit(solution)/shard_map/all_gather | solution.py:118
  31.2 10.6 %collective-permute-start.1 = (f32[8,4,2,480]{3,1,2,0:T(4,128)S(1)}, f32[8,4,2,480]{3,1,2,0:T(4,128)S(1)}, u32[]{:S(2)}, u32[]{:S(2)}) collective-permute-start(f32[8,4,2,480]{3,1,2,0:T(4,128)S(1)} %all_gather.30), channel_id=1, source_target_pairs={{8,0},{16,8},{24,16},{32,24},{40,32},{48,40},{56,48},{64,56},{72,6... | collective-permute-start | bytes 368648 | tf_op jit(solution)/shard_map/ppermute | solution.py:26
  41.9 1.9 collective-permute-start
  56.6 0.7 fusion.182
  58.0 1.0 fusion.21
  60.0 24.6 %all_gather.31 = f32[8,3,480]{2,1,0:T(4,128)S(1)} all-gather(f32[1,3,480]{2,1,0:T(4,128)S(1)} %reshape.1562), channel_id=1, replica_groups=mesh['tiles'=128,'sub'=8] {'sub'}, dimensions={0}, use_global_device_ids=true | all-gather | bytes 51840 | tf_op jit(solution)/shard_map/all_gather | solution.py:129
  84.5 1.9 collective-permute-start.2
  86.5 7.0 %collective-permute-start.3 = (f32[8,3,480]{2,1,0:T(4,128)S(1)}, f32[8,3,480]{2,1,0:T(4,128)S(1)}, u32[]{:S(2)}, u32[]{:S(2)}) collective-permute-start(f32[8,3,480]{2,1,0:T(4,128)S(1)} %all_gather.31), channel_id=1, source_target_pairs={{8,0},{16,8},{24,16},{32,24},{40,32},{48,40},{56,48},{64,56},{72,6... | collective-permute-start | bytes 138248 | tf_op jit(solution)/shard_map/ppermute | solution.py:26
  93.6 1.8 collective-permute-done.3
  100.1 24.6 %all_gather.32 = f32[8,3,480]{2,1,0:T(4,128)S(1)} all-gather(f32[1,3,480]{2,1,0:T(4,128)S(1)} %reshape.1563), channel_id=1, replica_groups=mesh['tiles'=128,'sub'=8] {'sub'}, dimensions={0}, use_global_device_ids=true | all-gather | bytes 51840 | tf_op jit(solution)/shard_map/all_gather | solution.py:129
  124.6 1.9 collective-permute-start.4
  126.6 7.0 %collective-permute-start.5 = (f32[8,3,480]{2,1,0:T(4,128)S(1)}, f32[8,3,480]{2,1,0:T(4,128)S(1)}, u32[]{:S(2)}, u32[]{:S(2)}) collective-permute-start(f32[8,3,480]{2,1,0:T(4,128)S(1)} %all_gather.32), channel_id=1, source_target_pairs={{8,0},{16,8},{24,16},{32,24},{40,32},{48,40},{56,48},{64,56},{72,6... | collective-permute-start | bytes 138248 | tf_op jit(solution)/shard_map/ppermute | solution.py:26
  133.6 1.8 collective-permute-done.5
  140.1 24.6 %all_gather.33 = f32[8,3,480]{2,1,0:T(4,128)S(1)} all-gather(f32[1,3,480]{2,1,0:T(4,128)S(1)} %reshape.1564), channel_id=1, replica_groups=mesh['tiles'=128,'sub'=8] {'sub'}, dimensions={0}, use_global_device_ids=true | all-gather | bytes 51840 | tf_op jit(solution)/shard_map/all_gather | solution.py:129
  164.7 1.9 collective-permute-start.6
  166.6 7.0 %collective-permute-start.7 = (f32[8,3,480]{2,1,0:T(4,128)S(1)}, f32[8,3,480]{2,1,0:T(4,128)S(1)}, u32[]{:S(2)}, u32[]{:S(2)}) collective-permute-start(f32[8,3,480]{2,1,0:T(4,128)S(1)} %all_gather.33), channel_id=1, source_target_pairs={{8,0},{16,8},{24,16},{32,24},{40,32},{48,40},{56,48},{64,56},{72,6... | collective-permute-start | bytes 138248 | tf_op jit(solution)/shard_map/ppermute | solution.py:26
  173.6 1.8 collective-permute-done.7
  180.1 24.6 %all_gather.34 = f32[8,3,480]{2,1,0:T(4,128)S(1)} all-gather(f32[1,3,480]{2,1,0:T(4,128)S(1)} %reshape.1565), channel_id=1, replica_groups=mesh['tiles'=128,'sub'=8] {'sub'}, dimensions={0}, use_global_device_ids=true | all-gather | bytes 51840 | tf_op jit(solution)/shard_map/all_gather | solution.py:129
  204.7 1.9 collective-permute-start.8
  206.6 7.0 %collective-permute-start.9 = (f32[8,3,480]{2,1,0:T(4,128)S(1)}, f32[8,3,480]{2,1,0:T(4,128)S(1)}, u32[]{:S(2)}, u32[]{:S(2)}) collective-permute-start(f32[8,3,480]{2,1,0:T(4,128)S(1)} %all_gather.34), channel_id=1, source_target_pairs={{8,0},{16,8},{24,16},{32,24},{40,32},{48,40},{56,48},{64,56},{72,6... | collective-permute-start | bytes 138248 | tf_op jit(solution)/shard_map/ppermute | solution.py:26
  213.6 1.8 collective-permute-done.9
  220.7 24.6 %all_gather.35 = f32[8,4,2,480]{3,1,2,0:T(4,128)S(1)} all-gather(f32[1,4,2,480]{3,1,2,0:T(4,128)S(1)} %reshape.1566), channel_id=1, replica_groups=mesh['tiles'=128,'sub'=8] {'sub'}, dimensions={0}, use_global_device_ids=true | all-gather | bytes 138240 | tf_op jit(solution)/shard_map/all_gather | solution.py:118
  245.3 1.9 collective-permute-start.11
  247.2 2.6 collective-permute-start.10
  249.9 7.0 %collective-permute-done.10 = f32[8,4,2,480]{3,1,2,0:T(4,128)S(1)} collective-permute-done((f32[8,4,2,480]{3,1,2,0:T(4,128)S(1)}, f32[8,4,2,480]{3,1,2,0:T(4,128)S(1)}, u32[]{:S(2)}, u32[]{:S(2)}) %collective-permute-start.10) | collective-permute-done | bytes 122912 | tf_op jit(solution)/shard_map/ppermute | solution.py:25
  257.1 0.7 fusion.177
  257.9 0.7 fusion.178
  261.2 1.0 fusion.31
  263.2 24.6 %all_gather.36 = f32[8,3,480]{2,1,0:T(4,128)S(1)} all-gather(f32[1,3,480]{2,1,0:T(4,128)S(1)} %reshape.1571), channel_id=1, replica_groups=mesh['tiles'=128,'sub'=8] {'sub'}, dimensions={0}, use_global_device_ids=true | all-gather | bytes 51840 | tf_op jit(solution)/shard_map/all_gather | solution.py:129
  287.7 1.9 collective-permute-start.12
  289.6 7.0 %collective-permute-start.13 = (f32[8,3,480]{2,1,0:T(4,128)S(1)}, f32[8,3,480]{2,1,0:T(4,128)S(1)}, u32[]{:S(2)}, u32[]{:S(2)}) collective-permute-start(f32[8,3,480]{2,1,0:T(4,128)S(1)} %all_gather.36), channel_id=1, source_target_pairs={{8,0},{16,8},{24,16},{32,24},{40,32},{48,40},{56,48},{64,56},{72,6... | collective-permute-start | bytes 138248 | tf_op jit(solution)/shard_map/ppermute | solution.py:26
  296.7 1.8 collective-permute-done.13
  303.2 24.6 %all_gather.37 = f32[8,3,480]{2,1,0:T(4,128)S(1)} all-gather(f32[1,3,480]{2,1,0:T(4,128)S(1)} %reshape.1572), channel_id=1, replica_groups=mesh['tiles'=128,'sub'=8] {'sub'}, dimensions={0}, use_global_device_ids=true | all-gather | bytes 51840 | tf_op jit(solution)/shard_map/all_gather | solution.py:129
  327.7 1.9 collective-permute-start.14
  329.7 7.0 %collective-permute-start.15 = (f32[8,3,480]{2,1,0:T(4,128)S(1)}, f32[8,3,480]{2,1,0:T(4,128)S(1)}, u32[]{:S(2)}, u32[]{:S(2)}) collective-permute-start(f32[8,3,480]{2,1,0:T(4,128)S(1)} %all_gather.37), channel_id=1, source_target_pairs={{8,0},{16,8},{24,16},{32,24},{40,32},{48,40},{56,48},{64,56},{72,6... | collective-permute-start | bytes 138248 | tf_op jit(solution)/shard_map/ppermute | solution.py:26
  336.7 1.8 collective-permute-done.15
  343.2 24.6 %all_gather.38 = f32[8,3,480]{2,1,0:T(4,128)S(1)} all-gather(f32[1,3,480]{2,1,0:T(4,128)S(1)} %reshape.1573), channel_id=1, replica_groups=mesh['tiles'=128,'sub'=8] {'sub'}, dimensions={0}, use_global_device_ids=true | all-gather | bytes 51840 | tf_op jit(solution)/shard_map/all_gather | solution.py:129
  367.7 1.9 collective-permute-start.16
  369.7 7.0 %collective-permute-start.17 = (f32[8,3,480]{2,1,0:T(4,128)S(1)}, f32[8,3,480]{2,1,0:T(4,128)S(1)}, u32[]{:S(2)}, u32[]{:S(2)}) collective-permute-start(f32[8,3,480]{2,1,0:T(4,128)S(1)} %all_gather.38), channel_id=1, source_target_pairs={{8,0},{16,8},{24,16},{32,24},{40,32},{48,40},{56,48},{64,56},{72,6... | collective-permute-start | bytes 138248 | tf_op jit(solution)/shard_map/ppermute | solution.py:26
  376.7 1.8 collective-permute-done.17
  383.2 24.6 %all_gather.39 = f32[8,3,480]{2,1,0:T(4,128)S(1)} all-gather(f32[1,3,480]{2,1,0:T(4,128)S(1)} %reshape.1574), channel_id=1, replica_groups=mesh['tiles'=128,'sub'=8] {'sub'}, dimensions={0}, use_global_device_ids=true | all-gather | bytes 51840 | tf_op jit(solution)/shard_map/all_gather | solution.py:129
  407.8 1.9 collective-permute-start.18
  409.8 7.0 %collective-permute-start.19 = (f32[8,3,480]{2,1,0:T(4,128)S(1)}, f32[8,3,480]{2,1,0:T(4,128)S(1)}, u32[]{:S(2)}, u32[]{:S(2)}) collective-permute-start(f32[8,3,480]{2,1,0:T(4,128)S(1)} %all_gather.39), channel_id=1, source_target_pairs={{8,0},{16,8},{24,16},{32,24},{40,32},{48,40},{56,48},{64,56},{72,6... | collective-permute-start | bytes 138248 | tf_op jit(solution)/shard_map/ppermute | solution.py:26
  416.9 1.8 collective-permute-done.19
  422.4 0.7 reshape.1116
  423.4 0.7 pad_maximum_fusion.79
  (331 shorter events, 48.8 us)
Async XLA Ops:
  31.2 22.5 %collective-permute-start.1 = (f32[8,4,2,480]{3,1,2,0:T(4,128)S(1)}, f32[8,4,2,480]{3,1,2,0:T(4,128)S(1)}, u32[]{:S(2)}, u32[]{:S(2)}) collective-permute-start(f32[8,4,2,480]{3,1,2,0:T(4,128)S(1)} %all_gather.30), channel_id=1, source_target_pairs={{8,0},{16,8},{24,16},{32,24},{40,32},{48,40},{56,48},{64,56},{72,6... | collective-permute-start | bytes 368648 | tf_op jit(solution)/shard_map/ppermute | solution.py:26
  41.9 11.8 %collective-permute-start = (f32[8,4,2,480]{3,1,2,0:T(4,128)S(1)}, f32[8,4,2,480]{3,1,2,0:T(4,128)S(1)}, u32[]{:S(2)}, u32[]{:S(2)}) collective-permute-start(f32[8,4,2,480]{3,1,2,0:T(4,128)S(1)} %all_gather.30), channel_id=1, source_target_pairs={{0,8},{8,16},{16,24},{24,32},{32,40},{40,48},{48,56},{56,64},{64,7... | collective-permute-start | bytes 368648 | tf_op jit(solution)/shard_map/ppermute | solution.py:25
  43.8 0.7 copy-start
  84.5 9.0 %collective-permute-start.2 = (f32[8,3,480]{2,1,0:T(4,128)S(1)}, f32[8,3,480]{2,1,0:T(4,128)S(1)}, u32[]{:S(2)}, u32[]{:S(2)}) collective-permute-start(f32[8,3,480]{2,1,0:T(4,128)S(1)} %all_gather.31), channel_id=1, source_target_pairs={{0,8},{8,16},{16,24},{24,32},{32,40},{40,48},{48,56},{56,64},{64,7... | collective-permute-start | bytes 138248 | tf_op jit(solution)/shard_map/ppermute | solution.py:25
  86.5 8.9 %collective-permute-start.3 = (f32[8,3,480]{2,1,0:T(4,128)S(1)}, f32[8,3,480]{2,1,0:T(4,128)S(1)}, u32[]{:S(2)}, u32[]{:S(2)}) collective-permute-start(f32[8,3,480]{2,1,0:T(4,128)S(1)} %all_gather.31), channel_id=1, source_target_pairs={{8,0},{16,8},{24,16},{32,24},{40,32},{48,40},{56,48},{64,56},{72,6... | collective-permute-start | bytes 138248 | tf_op jit(solution)/shard_map/ppermute | solution.py:26
  124.6 8.9 %collective-permute-start.4 = (f32[8,3,480]{2,1,0:T(4,128)S(1)}, f32[8,3,480]{2,1,0:T(4,128)S(1)}, u32[]{:S(2)}, u32[]{:S(2)}) collective-permute-start(f32[8,3,480]{2,1,0:T(4,128)S(1)} %all_gather.32), channel_id=1, source_target_pairs={{0,8},{8,16},{16,24},{24,32},{32,40},{40,48},{48,56},{56,64},{64,7... | collective-permute-start | bytes 138248 | tf_op jit(solution)/shard_map/ppermute | solution.py:25
  126.6 8.9 %collective-permute-start.5 = (f32[8,3,480]{2,1,0:T(4,128)S(1)}, f32[8,3,480]{2,1,0:T(4,128)S(1)}, u32[]{:S(2)}, u32[]{:S(2)}) collective-permute-start(f32[8,3,480]{2,1,0:T(4,128)S(1)} %all_gather.32), channel_id=1, source_target_pairs={{8,0},{16,8},{24,16},{32,24},{40,32},{48,40},{56,48},{64,56},{72,6... | collective-permute-start | bytes 138248 | tf_op jit(solution)/shard_map/ppermute | solution.py:26
  164.7 8.9 %collective-permute-start.6 = (f32[8,3,480]{2,1,0:T(4,128)S(1)}, f32[8,3,480]{2,1,0:T(4,128)S(1)}, u32[]{:S(2)}, u32[]{:S(2)}) collective-permute-start(f32[8,3,480]{2,1,0:T(4,128)S(1)} %all_gather.33), channel_id=1, source_target_pairs={{0,8},{8,16},{16,24},{24,32},{32,40},{40,48},{48,56},{56,64},{64,7... | collective-permute-start | bytes 138248 | tf_op jit(solution)/shard_map/ppermute | solution.py:25
  166.6 8.9 %collective-permute-start.7 = (f32[8,3,480]{2,1,0:T(4,128)S(1)}, f32[8,3,480]{2,1,0:T(4,128)S(1)}, u32[]{:S(2)}, u32[]{:S(2)}) collective-permute-start(f32[8,3,480]{2,1,0:T(4,128)S(1)} %all_gather.33), channel_id=1, source_target_pairs={{8,0},{16,8},{24,16},{32,24},{40,32},{48,40},{56,48},{64,56},{72,6... | collective-permute-start | bytes 138248 | tf_op jit(solution)/shard_map/ppermute | solution.py:26
  204.7 8.9 %collective-permute-start.8 = (f32[8,3,480]{2,1,0:T(4,128)S(1)}, f32[8,3,480]{2,1,0:T(4,128)S(1)}, u32[]{:S(2)}, u32[]{:S(2)}) collective-permute-start(f32[8,3,480]{2,1,0:T(4,128)S(1)} %all_gather.34), channel_id=1, source_target_pairs={{0,8},{8,16},{16,24},{24,32},{32,40},{40,48},{48,56},{56,64},{64,7... | collective-permute-start | bytes 138248 | tf_op jit(solution)/shard_map/ppermute | solution.py:25
  206.6 8.9 %collective-permute-start.9 = (f32[8,3,480]{2,1,0:T(4,128)S(1)}, f32[8,3,480]{2,1,0:T(4,128)S(1)}, u32[]{:S(2)}, u32[]{:S(2)}) collective-permute-start(f32[8,3,480]{2,1,0:T(4,128)S(1)} %all_gather.34), channel_id=1, source_target_pairs={{8,0},{16,8},{24,16},{32,24},{40,32},{48,40},{56,48},{64,56},{72,6... | collective-permute-start | bytes 138248 | tf_op jit(solution)/shard_map/ppermute | solution.py:26
  245.3 11.6 %collective-permute-start.11 = (f32[8,4,2,480]{3,1,2,0:T(4,128)S(1)}, f32[8,4,2,480]{3,1,2,0:T(4,128)S(1)}, u32[]{:S(2)}, u32[]{:S(2)}) collective-permute-start(f32[8,4,2,480]{3,1,2,0:T(4,128)S(1)} %all_gather.35), channel_id=1, source_target_pairs={{8,0},{16,8},{24,16},{32,24},{40,32},{48,40},{56,48},{64,56},{72,6... | collective-permute-start | bytes 368648 | tf_op jit(solution)/shard_map/ppermute | solution.py:26
  247.2 9.6 %collective-permute-start.10 = (f32[8,4,2,480]{3,1,2,0:T(4,128)S(1)}, f32[8,4,2,480]{3,1,2,0:T(4,128)S(1)}, u32[]{:S(2)}, u32[]{:S(2)}) collective-permute-start(f32[8,4,2,480]{3,1,2,0:T(4,128)S(1)} %all_gather.35), channel_id=1, source_target_pairs={{0,8},{8,16},{16,24},{24,32},{32,40},{40,48},{48,56},{56,64},{64,7... | collective-permute-start | bytes 368648 | tf_op jit(solution)/shard_map/ppermute | solution.py:25
  287.7 8.9 %collective-permute-start.12 = (f32[8,3,480]{2,1,0:T(4,128)S(1)}, f32[8,3,480]{2,1,0:T(4,128)S(1)}, u32[]{:S(2)}, u32[]{:S(2)}) collective-permute-start(f32[8,3,480]{2,1,0:T(4,128)S(1)} %all_gather.36), channel_id=1, source_target_pairs={{0,8},{8,16},{16,24},{24,32},{32,40},{40,48},{48,56},{56,64},{64,7... | collective-permute-start | bytes 138248 | tf_op jit(solution)/shard_map/ppermute | solution.py:25
  289.6 8.9 %collective-permute-start.13 = (f32[8,3,480]{2,1,0:T(4,128)S(1)}, f32[8,3,480]{2,1,0:T(4,128)S(1)}, u32[]{:S(2)}, u32[]{:S(2)}) collective-permute-start(f32[8,3,480]{2,1,0:T(4,128)S(1)} %all_gather.36), channel_id=1, source_target_pairs={{8,0},{16,8},{24,16},{32,24},{40,32},{48,40},{56,48},{64,56},{72,6... | collective-permute-start | bytes 138248 | tf_op jit(solution)/shard_map/ppermute | solution.py:26
  327.7 8.9 %collective-permute-start.14 = (f32[8,3,480]{2,1,0:T(4,128)S(1)}, f32[8,3,480]{2,1,0:T(4,128)S(1)}, u32[]{:S(2)}, u32[]{:S(2)}) collective-permute-start(f32[8,3,480]{2,1,0:T(4,128)S(1)} %all_gather.37), channel_id=1, source_target_pairs={{0,8},{8,16},{16,24},{24,32},{32,40},{40,48},{48,56},{56,64},{64,7... | collective-permute-start | bytes 138248 | tf_op jit(solution)/shard_map/ppermute | solution.py:25
  329.7 8.9 %collective-permute-start.15 = (f32[8,3,480]{2,1,0:T(4,128)S(1)}, f32[8,3,480]{2,1,0:T(4,128)S(1)}, u32[]{:S(2)}, u32[]{:S(2)}) collective-permute-start(f32[8,3,480]{2,1,0:T(4,128)S(1)} %all_gather.37), channel_id=1, source_target_pairs={{8,0},{16,8},{24,16},{32,24},{40,32},{48,40},{56,48},{64,56},{72,6... | collective-permute-start | bytes 138248 | tf_op jit(solution)/shard_map/ppermute | solution.py:26
  367.7 8.9 %collective-permute-start.16 = (f32[8,3,480]{2,1,0:T(4,128)S(1)}, f32[8,3,480]{2,1,0:T(4,128)S(1)}, u32[]{:S(2)}, u32[]{:S(2)}) collective-permute-start(f32[8,3,480]{2,1,0:T(4,128)S(1)} %all_gather.38), channel_id=1, source_target_pairs={{0,8},{8,16},{16,24},{24,32},{32,40},{40,48},{48,56},{56,64},{64,7... | collective-permute-start | bytes 138248 | tf_op jit(solution)/shard_map/ppermute | solution.py:25
  369.7 8.9 %collective-permute-start.17 = (f32[8,3,480]{2,1,0:T(4,128)S(1)}, f32[8,3,480]{2,1,0:T(4,128)S(1)}, u32[]{:S(2)}, u32[]{:S(2)}) collective-permute-start(f32[8,3,480]{2,1,0:T(4,128)S(1)} %all_gather.38), channel_id=1, source_target_pairs={{8,0},{16,8},{24,16},{32,24},{40,32},{48,40},{56,48},{64,56},{72,6... | collective-permute-start | bytes 138248 | tf_op jit(solution)/shard_map/ppermute | solution.py:26
  407.8 9.1 %collective-permute-start.18 = (f32[8,3,480]{2,1,0:T(4,128)S(1)}, f32[8,3,480]{2,1,0:T(4,128)S(1)}, u32[]{:S(2)}, u32[]{:S(2)}) collective-permute-start(f32[8,3,480]{2,1,0:T(4,128)S(1)} %all_gather.39), channel_id=1, source_target_pairs={{0,8},{8,16},{16,24},{24,32},{32,40},{40,48},{48,56},{56,64},{64,7... | collective-permute-start | bytes 138248 | tf_op jit(solution)/shard_map/ppermute | solution.py:25
  409.8 8.9 %collective-permute-start.19 = (f32[8,3,480]{2,1,0:T(4,128)S(1)}, f32[8,3,480]{2,1,0:T(4,128)S(1)}, u32[]{:S(2)}, u32[]{:S(2)}) collective-permute-start(f32[8,3,480]{2,1,0:T(4,128)S(1)} %all_gather.39), channel_id=1, source_target_pairs={{8,0},{16,8},{24,16},{32,24},{40,32},{48,40},{56,48},{64,56},{72,6... | collective-permute-start | bytes 138248 | tf_op jit(solution)/shard_map/ppermute | solution.py:26
where the time goes:
time: 426 us; the launch traced here: 424 us
  blocking collectives  248 us (58%)
  starting transfers between devices  88 us (21%)
  other arithmetic  34.3 us (8%)
  local copies, waits for them, and re-layouts  21.9 us (5%)
  waiting for transfers between devices  21.6 us (5%)
  between operations  10.3 us (2%)
    all_gather x8, blocking collectives, surface_halos(): group = lax.all_gather(panels, 'sub', axis=0, tiled=True)  196 us
    ppermute x10, starting transfers between devices, padded_2(): after = lax.ppermute(leading, axis, down)  68.2 us
    all_gather x2, blocking collectives, clinic_halos(): group = lax.all_gather(panels, 'sub', axis=0, tiled=True)  51.5 us
    ppermute x10, starting transfers between devices, padded_2(): before = lax.ppermute(last, axis, up)  19.8 us
    select_n x30, other arithmetic, pick(): result.append(jnp.where(keep, rows, jnp.zeros_like(rows)))  19.4 us
    ppermute x10, waiting for transfers between devices, padded_2(): after = lax.ppermute(leading, axis, down)  14.6 us
  transfers between devices with their start and end apart: 20, of which 9 were waited for; matrix products, arithmetic and copies ran while one was open for 0% of the time, Pallas kernels for 0%

commit v1 on v0

v1 whole, which is shorter than its diff:
```python
import functools

import jax
import jax.numpy as jnp
from jax import lax
from jax.experimental import pallas as pl
from jax.experimental.pallas import tpu as pltpu
from jax.sharding import PartitionSpec as P

MESH = pl.DeviceIdType.MESH
TILE = 60
STEPS = 2
SUBCYCLES = 4
SUB = 8

time_step = 0.2
mixing = 0.02
coriolis = 0.5
gravity_step = 0.25
depth_step = 0.25

TOP = 24
ROWS = 112
ETA, WET = 8, 9
ITEMS = (
    [(4 + i, 18 * i, 18) for i in range(4)]
    + [(ETA, 72, 16), (WET, 88, 16)]
    + [(i, 104 + 4 * i, 4) for i in range(4)]
)


def lanes(shape):
    return lax.broadcasted_iota(jnp.int32, shape, len(shape) - 1)


def turn(x, shift):
    shift %= 128
    return pltpu.roll(x, shift, x.ndim - 1) if shift else x


def within(lane, first, count):
    return (lane >= first) & (lane < first + count)


def pack(D, p1):
    def both(item, north, south, count):
        return D[item, TOP + north : TOP + north + count] + turn(D[item, TOP + south : TOP + south + count], 64)

    for i in range(4):
        p1[i, 0:16] = both(4 + i, 0, 42, 16)
        p1[6, 4 * i : 4 * i + 4] = both(i, 0, 56, 4)
        p1[7, 2 * i : 2 * i + 2] = both(4 + i, 16, 58, 2)
    p1[4, 0:16] = both(ETA, 0, 44, 16)
    p1[5, 0:16] = both(WET, 0, 44, 16)
    p1[7, 8:16] = jnp.zeros((8, 128), jnp.float32)
    lane = lanes((64, 128))
    east = west = jnp.zeros((64, 128), jnp.float32)
    for item, first, depth in ITEMS:
        whole = D[item, TOP : TOP + 64]
        here = within(lane, first, depth)
        east = jnp.where(here, turn(whole, first - (TILE - depth)), east)
        west = jnp.where(here, turn(whole, first), west)
    for m in range(SUB):
        p1[m, 16:24] = east[8 * m : 8 * m + 8]
        p1[m, 24:32] = west[8 * m : 8 * m + 8]


def take(table, index):
    out = jnp.full((SUB, 128), -1, jnp.int32)
    for k in range(SUB):
        out = jnp.where(index == k, jnp.broadcast_to(table[k : k + 1], (SUB, 128)), out)
    return out


def wanted(ids, me, lists):
    def side(column, direction):
        return jnp.concatenate([ids[column, r, direction : direction + 1] for r in range(SUB)], 0)

    north, south = side(1, 0), side(1, 2)
    lists[0] = jnp.where(lanes((SUB, 128)) < 64, south, north)
    for at, column, direction in ((1, 2, 3), (3, 0, 1)):
        beside, above, below = side(column, direction), side(column, 0), side(column, 2)
        up = jnp.where(above >= 0, take(beside, above), take(north, beside))
        down = jnp.where(below >= 0, take(beside, below), take(south, beside))
        lists[at] = beside
        lists[at + 1] = jnp.where(me >= 4, up, down)


def unpack(D, rns, re, rw, eb, wb):
    for held, got in ((eb, re), (wb, rw)):
        for j in range(3):
            held[4 + 8 * j : 12 + 8 * j] = got[5 + j, 8:16]
        for m in range(SUB):
            held[TOP + 8 * m : TOP + 8 * m + 8] = got[m, 0:8]
        for j in range(3):
            held[84 + 8 * j : 92 + 8 * j] = got[j, 8:16]

    for item, first, depth in ITEMS:
        begin, count = TOP - depth, TILE + 2 * depth
        lane = lanes((count, 128))
        east = turn(eb[begin : begin + count], TILE - first)
        west = turn(wb[begin : begin + count], 128 - depth - first)
        sides = jnp.where(within(lane, TILE, depth), east, jnp.where(lane >= 128 - depth, west, 0.0))
        D[item, begin : begin + count] = D[item, begin : begin + count] + sides

    def put(item, rows, north, south):
        count = rows.shape[0]
        tile = lanes((count, 128)) < TILE
        D[item, TOP + north : TOP + north + count] += jnp.where(tile, turn(rows, 64), 0.0)
        D[item, TOP + south : TOP + south + count] += jnp.where(tile, rows, 0.0)

    for i in range(4):
        put(4 + i, rns[i], -18, 60)
        put(4 + i, rns[7, 2 * i : 2 * i + 2], -2, 76)
        put(i, rns[6, 4 * i : 4 * i + 4], -4, 60)
    put(ETA, rns[4], -16, 60)
    put(WET, rns[5], -16, 60)


def clinic(D, N, item, begin, count):
    level = item % 2

    def at(which, shift=0):
        return D[which, begin + shift : begin + shift + count]

    mid, north, south = at(item), at(item, -1), at(item, 1)
    wet = at(WET)
    u, v = at(4 + level), at(6 + level)
    right, left = turn(mid, -1), turn(mid, 1)
    cross = 2.0 * (north + south) - 8.0 * mid
    smooth = (
        20.0 * mid
        - 8.0 * (north + south)
        + at(item, -2)
        + at(item, 2)
        + turn(cross + right, -1)
        + turn(cross + left, 1)
    )
    tend = -(u * ((right - left) * 0.5) + v * ((south - north) * 0.5)) - mixing * smooth
    if item // 2 == 2:
        tend = tend + coriolis * v
    if item // 2 == 3:
        tend = tend - coriolis * u
    N[item, begin : begin + count] = (mid + time_step * tend) * wet
    lane = lanes((2, 128))
    for row in (TOP - 1, TOP + TILE - 1):
        swapped = jnp.concatenate([D[item, row + 1 : row + 2], D[item, row : row + 1]], 0)
        diagonal = jnp.where(
            (lane == 0) | (lane == TILE),
            turn(swapped, 1),
            jnp.where((lane == 127) | (lane == TILE - 1), turn(swapped, -1), 0.0),
        )
        N[item, row : row + 2] += (2.0 * time_step * mixing) * diagonal * D[WET, row : row + 2]


def tropic(heights, norths, wet_at, eta, zonal, meridional, begin, count):
    for _ in range(SUBCYCLES):
        heights[begin : begin + count] = eta
        norths[begin : begin + count] = meridional

        def a(shift):
            return heights[begin + shift : begin + shift + count]

        def c(shift):
            return norths[begin + shift : begin + shift + count]

        new_u = zonal - (gravity_step * 0.5) * (turn(eta, -1) - turn(eta, 1))
        new_v = meridional - (gravity_step * 0.5) * (a(1) - a(-1))
        along = (c(1) - c(-1)) - (gravity_step * 0.5) * ((a(2) - eta) - (eta - a(-2)))
        spread = (turn(new_u, -1) - turn(new_u, 1)) + along
        wet = wet_at(begin, count)
        eta = (eta - (depth_step * 0.5) * spread) * wet
        zonal, meridional = new_u * wet, new_v * wet
    return eta, zonal, meridional


def kernel(
    columns,
    near,
    state,
    surface,
    wet,
    new_state,
    new_surface,
    D,
    N,
    heights,
    norths,
    p1,
    c1,
    my_ids,
    ids,
    lists,
    out_own,
    out_up,
    out_down,
    rns,
    re,
    rw,
    eb,
    wb,
    sent,
    came,
):
    column, me = lax.axis_index("tiles"), lax.axis_index("sub")
    after, before = lax.rem(column + 1, columns), lax.rem(column + columns - 1, columns)
    others = [lax.rem(me + k, SUB) for k in range(SUB)]
    own = [(column, r) for r in others[1:]]
    ups = [(after, r) for r in others]
    downs = [(before, r) for r in others]

    barrier = pltpu.get_barrier_semaphore()
    for device in own + ups + downs:
        pl.semaphore_signal(barrier, inc=1, device_id=device, device_id_type=MESH)

    row = lax.broadcasted_iota(jnp.int32, (SUB, 128), 0)
    mine = jnp.full((SUB, 128), -1, jnp.int32)
    for direction, base in enumerate((column, column + 1, column, column - 1)):
        listed = near[0, direction]
        slot = jnp.where(listed >= 0, listed - base * SUB, -1)
        mine = jnp.where(row == direction, slot, mine)
    my_ids[...] = mine
    ids[1, me] = mine

    D[...] = jnp.zeros_like(D)
    ocean = wet[...]
    D[WET, TOP : TOP + TILE, 0:TILE] = ocean
    D[ETA, TOP : TOP + TILE, 0:TILE] = surface[...] * ocean
    for item in range(8):
        D[item, TOP : TOP + TILE, 0:TILE] = state[item] * ocean
    pack(D, p1)
    c1[me] = p1[me]

    def send(source, target, kind, device):
        pltpu.make_async_remote_copy(
            src_ref=source,
            dst_ref=target,
            send_sem=sent.at[kind],
            recv_sem=came.at[kind],
            device_id=device,
            device_id_type=MESH,
        ).start()

    pl.semaphore_wait(barrier, len(own + ups + downs))
    for device in own:
        send(p1.at[device[1]], c1.at[me], 0, device)
    for device in own:
        send(my_ids, ids.at[1, me], 1, device)
    for device in ups:
        send(my_ids, ids.at[0, me], 2, device)
    for device in downs:
        send(my_ids, ids.at[2, me], 3, device)

    def wait(ref, semaphore):
        pltpu.make_async_copy(ref, ref, semaphore).wait()

    seven, eight = pl.ds(0, SUB - 1), pl.ds(0, SUB)
    wait(ids.at[1, seven], came.at[1])
    wait(ids.at[0, eight], came.at[2])
    wait(ids.at[2, eight], came.at[3])
    wanted(ids, me, lists)
    wait(c1.at[seven], came.at[0])

    def picked(which, r, first, count):
        want = jnp.broadcast_to(lists[which, pl.ds(r, 1)], (8, 128))
        outs = [jnp.zeros((8, 128), jnp.float32) for _ in range(count // 8)]
        for k in range(SUB):
            hit = want == k
            for i in range(count // 8):
                outs[i] = jnp.where(hit, c1[k, first + 8 * i : first + 8 * i + 8], outs[i])
        return outs

    for k in range(SUB):
        r = others[k]
        parts = picked(0, r, 0, 16)
        for at in range(2):
            if k:
                out_own[r, 8 * at : 8 * at + 8] = parts[at]
            else:
                rns[me, 8 * at : 8 * at + 8] = parts[at]
        if k:
            send(out_own.at[r], rns.at[me], 4, (column, r))
        out_up[r, 0:8] = picked(1, r, 16, 8)[0]
        out_up[r, 8:16] = picked(2, r, 16, 8)[0]
        send(out_up.at[r], rw.at[me], 5, (after, r))
        out_down[r, 0:8] = picked(3, r, 24, 8)[0]
        out_down[r, 8:16] = picked(4, r, 24, 8)[0]
        send(out_down.at[r], re.at[me], 6, (before, r))

    wait(rns.at[seven], came.at[4])
    wait(rw.at[eight], came.at[5])
    wait(re.at[eight], came.at[6])

    unpack(D, rns, re, rw, eb, wb)
    N[...] = jnp.zeros_like(N)
    heights[...] = jnp.zeros_like(heights)
    norths[...] = jnp.zeros_like(norths)
    weights = (2.0 / 6.0, 4.0 / 6.0)
    fields, other = D, N
    wet_at = lambda begin, count: D[WET, begin : begin + count]
    for step in range(STEPS):
        begin, count = ((8, 96), (16, 80))[step]
        tracer = ((16, 72), (24, 64))[step]
        for item in range(4):
            clinic(fields, other, item, *tracer)
        for item in range(4, 8):
            clinic(fields, other, item, begin, count)
        rows = slice(begin, begin + count)
        old_u = weights[0] * other[4, rows] + weights[1] * other[5, rows]
        old_v = weights[0] * other[6, rows] + weights[1] * other[7, rows]
        eta, zonal, meridional = tropic(heights, norths, wet_at, fields[ETA, rows], old_u, old_v, begin, count)
        other[ETA, rows] = eta
        other[WET] = fields[WET]
        for level in range(2):
            other[4 + level, rows] += zonal - old_u
            other[6 + level, rows] += meridional - old_v
        fields, other = other, fields

    for item in range(8):
        new_state[item] = fields[item, TOP : TOP + TILE, 0:TILE]
    new_surface[...] = fields[ETA, TOP : TOP + TILE, 0:TILE]

    wait(c1.at[seven], sent.at[0])
    wait(ids.at[1, seven], sent.at[1])
    wait(ids.at[0, eight], sent.at[2])
    wait(ids.at[2, eight], sent.at[3])
    wait(rns.at[seven], sent.at[4])
    wait(rw.at[eight], sent.at[5])
    wait(re.at[eight], sent.at[6])


def shards(columns, state, surface, land_mask, neighbours):
    wet = land_mask.reshape(TILE, TILE).astype(jnp.float32)
    vmem = pl.BlockSpec(memory_space=pltpu.VMEM)
    f32 = lambda *shape: pltpu.VMEM(shape, jnp.float32)
    new_state, new_surface = pl.pallas_call(
        functools.partial(kernel, columns),
        out_shape=(
            jax.ShapeDtypeStruct((8, TILE, TILE), jnp.float32),
            jax.ShapeDtypeStruct((TILE, TILE), jnp.float32),
        ),
        in_specs=[pl.BlockSpec(memory_space=pltpu.SMEM), vmem, vmem, vmem],
        out_specs=(vmem, vmem),
        scratch_shapes=[
            f32(10, ROWS, 128),
            f32(10, ROWS, 128),
            f32(ROWS, 128),
            f32(ROWS, 128),
            f32(SUB, 32, 128),
            f32(SUB, 32, 128),
            pltpu.VMEM((8, 128), jnp.int32),
            pltpu.VMEM((3, SUB, 8, 128), jnp.int32),
            pltpu.VMEM((5, 8, 128), jnp.int32),
        ]
        + [f32(SUB, 16, 128)] * 6
        + [f32(ROWS, 128)] * 2
        + [pltpu.SemaphoreType.DMA((7,)), pltpu.SemaphoreType.DMA((7,))],
        compiler_params=pltpu.CompilerParams(
            collective_id=0, has_side_effects=True, vmem_limit_bytes=32 * 1024 * 1024
        ),
    )(neighbours, state.reshape(8, TILE, TILE), surface.reshape(TILE, TILE), wet)
    return new_state.reshape(1, 4, 2, TILE * TILE), new_surface.reshape(1, TILE * TILE)


def solution(mesh):
    spec = P(("tiles", "sub"))
    return jax.shard_map(
        functools.partial(shards, mesh.shape["tiles"]),
        mesh=mesh,
        in_specs=(spec, spec, spec, spec),
        out_specs=(spec, spec),
        check_vma=False,
    )
```

time: 426 us -> 46.5 us (0.11)
  the two profiles are of different devices: /device:TPU:8 before, /device:TPU:1 now
where the time goes in v1:
time: 46.5 us; the launch traced here: 46.2 us
  Pallas kernels  41.5 us (89%)
  local copies, waits for them, and re-layouts  2.48 us (5%)
  other arithmetic  1.54 us (3%)
  between operations  0.69 us (1%)
    pallas_call x1, Pallas kernels, shards(): pl.pallas_call(functools.partial(kernel, columns), out_shape=(jax.ShapeDt...  41.5 us

profile of v1, /device:TPU:1, one launch (start us, length us, event | category | flops | bytes accessed | tf_op | source)
XLA Modules:
  0.0 46.2 jit_solution(16595585001131977528)
XLA Ops:
  0.6 0.0 copy-start.1
  0.6 0.8 %reduce = f32[3600]{0:T(1024)S(1)} reduce(f32[1,3600]{1,0:T(1,128)} %param.5, f32[]{:T(128)} %constant.4), dimensions={0}, to_apply=%param.5.reduce_sub_computation | reduce | bytes 28804 | tf_op args[1]
  1.4 0.1 reshape.19.surface
  1.5 0.8 %convert_reduce_fusion = f32[3600]{0:T(1024)S(1)} fusion(s32[1,3600]{1,0:T(1,128)} %param.6), kind=kLoop, calls=%fused_computation | loop fusion | flops 3600 | bytes 28800 | tf_op jit(solution)/shard_map/convert_element_type | solution.py:333
  2.3 0.1 convert_element_type.6.wet
  2.4 0.0 copy-done.1
  2.4 0.0 copy-start
  2.4 0.4 reshape.18.state
  2.8 0.3 copy-done
  3.1 41.5 %shard_map.59 = (f32[8,60,60]{2,1,0:T(8,128)S(1)}, f32[60,60]{1,0:T(8,128)S(1)}) custom-call(s32[1,4]{1,0:T(1,128)S(1)} %copy-done, f32[8,60,60]{2,1,0:T(8,128)S(1)} %reshape.18.state, f32[60,60]{1,0:T(8,128)S(1)} %reshape.19.surface, f32[60,60]{1,0:T(8,128)S(1)} %convert_element_type.6.wet), custom_call_target="tpu_custom_call" | custom-call | tf_op jit(solution)/shard_map/pallas_call | solution.py:336
  44.6 0.9 %reshape.20 = f32[1,4,2,3600]{3,2,1,0:T(2,128)} reshape(f32[8,60,60]{2,1,0:T(8,128)S(1)} %get-tuple-element.4) | data formatting | bytes 230400 | tf_op jit(solution)/shard_map/reshape | solution.py:362
  45.5 0.7 %reshape.21 = f32[1,3600]{1,0:T(1,128)} reshape(f32[60,60]{1,0:T(8,128)S(1)} %get-tuple-element.5) | data formatting | bytes 28800 | tf_op jit(solution)/shard_map/reshape | solution.py:362
Async XLA Ops:
  0.6 1.8 %copy-start.1 = (f32[1,4,2,3600]{3,2,1,0:T(2,128)S(1)}, f32[1,4,2,3600]{3,2,1,0:T(2,128)}, u32[]{:S(2)}) copy-start(f32[1,4,2,3600]{3,2,1,0:T(2,128)} %param.4) | copy-start | bytes 345604
  2.4 0.7 %copy-start = (s32[1,4]{1,0:T(1,128)S(1)}, s32[1,4]{1,0:T(1,128)}, u32[]{:S(2)}) copy-start(s32[1,4]{1,0:T(1,128)} %near.1) | copy-start | bytes 52

commit v2 on v1

v2 whole, which is shorter than its diff:
```python
import functools

import jax
import jax.numpy as jnp
from jax import lax
from jax.experimental import pallas as pl
from jax.experimental.pallas import tpu as pltpu
from jax.sharding import PartitionSpec as P

MESH = pl.DeviceIdType.MESH
TILE = 60
STEPS = 2
SUBCYCLES = 4
SUB = 8

time_step = 0.2
mixing = 0.02
coriolis = 0.5
gravity_step = 0.25
depth_step = 0.25

TOP = 24
ROWS = 112
ETA, WET = 8, 9
ITEMS = (
    [(4 + i, 17 * i, 17) for i in range(4)]
    + [(ETA, 68, 16), (WET, 84, 16)]
    + [(i, 100 + 4 * i, 4) for i in range(4)]
)
QUARTERS = (0, 16, 28, 44)


def lanes(shape):
    return lax.broadcasted_iota(jnp.int32, shape, len(shape) - 1)


def turn(x, shift):
    shift %= 128
    return pltpu.roll(x, shift, x.ndim - 1) if shift else x


def within(lane, first, count):
    return (lane >= first) & (lane < first + count)


def pack(D, ns, sides):
    def both(item, north, south, count):
        return D[item, TOP + north : TOP + north + count] + turn(D[item, TOP + south : TOP + south + count], 64)

    for i in range(4):
        ns[i, 0:16] = both(4 + i, 0, 43, 16)
        ns[6, 4 * i : 4 * i + 4] = both(i, 0, 56, 4)
        ns[7, i : i + 1] = both(4 + i, 16, 59, 1)
    ns[4, 0:16] = both(ETA, 0, 44, 16)
    ns[5, 0:16] = both(WET, 0, 44, 16)
    ns[7, 4:16] = jnp.zeros((12, 128), jnp.float32)
    lane = lanes((TILE, 128))
    east = west = jnp.zeros((TILE, 128), jnp.float32)
    for item, first, depth in ITEMS:
        whole = D[item, TOP : TOP + TILE]
        here = within(lane, first, depth)
        east = jnp.where(here, turn(whole, first - (TILE - depth)), east)
        west = jnp.where(here, turn(whole, first), west)
    for q, row in enumerate(QUARTERS):
        sides[0, q, 0:16] = east[row : row + 16]
        sides[1, q, 0:16] = west[row : row + 16]


def take(table, index):
    out = jnp.full((SUB, 128), -1.0, jnp.float32)
    for k in range(SUB):
        out = jnp.where(index == k, jnp.broadcast_to(table[k : k + 1], (SUB, 128)), out)
    return out


def wanted(own_in, side_in, me, lists):
    def column(held, direction):
        return jnp.concatenate([held[r, 16 + direction : 17 + direction] for r in range(SUB)], 0)

    north, east, south, west = (column(own_in, direction) for direction in range(4))
    beside = jnp.where(lax.rem(me, 2) == 0, east, west)
    up = jnp.where(north >= 0, take(beside, north), take(column(side_in, 0), beside))
    down = jnp.where(south >= 0, take(beside, south), take(column(side_in, 2), beside))
    lists[0] = jnp.where(lanes((SUB, 128)) < 64, south, north)
    lists[1] = beside
    lists[2] = jnp.where(me >= 4, up, down)


def unpack(D, got, eb, wb):
    for held, odd in ((eb, 0), (wb, 1)):
        held[8:24] = got[6 + odd, 32:48]
        for q, row in enumerate(QUARTERS):
            held[TOP + row : TOP + row + 16] = got[2 * q + odd, 16:32]
        held[84:100] = got[odd, 32:48]

    def put(item, rows, north, south):
        count = rows.shape[0]
        tile = lanes((count, 128)) < TILE
        D[item, TOP + north : TOP + north + count] = jnp.where(tile, turn(rows, 64), 0.0)
        D[item, TOP + south : TOP + south + count] = jnp.where(tile, rows, 0.0)

    for i in range(4):
        put(4 + i, got[i, 0:16], -17, 60)
        put(4 + i, got[7, i : i + 1], -1, 76)
        put(i, got[6, 4 * i : 4 * i + 4], -4, 60)
    put(ETA, got[4, 0:16], -16, 60)
    put(WET, got[5, 0:16], -16, 60)

    for item, first, depth in ITEMS:
        beyond = min(depth, 16)
        begin, count = TOP - beyond, TILE + 2 * beyond
        lane = lanes((count, 128))
        east = turn(eb[begin : begin + count], TILE - first)
        west = turn(wb[begin : begin + count], 128 - depth - first)
        sides = jnp.where(within(lane, TILE, depth), east, jnp.where(lane >= 128 - depth, west, 0.0))
        D[item, begin : begin + count] = D[item, begin : begin + count] + sides


def clinic(D, N, item, begin, count):
    level = item % 2

    def at(which, shift=0):
        return D[which, begin + shift : begin + shift + count]

    mid, north, south = at(item), at(item, -1), at(item, 1)
    wet = at(WET)
    u, v = at(4 + level), at(6 + level)
    right, left = turn(mid, -1), turn(mid, 1)
    cross = 2.0 * (north + south) - 8.0 * mid
    smooth = (
        20.0 * mid
        - 8.0 * (north + south)
        + at(item, -2)
        + at(item, 2)
        + turn(cross + right, -1)
        + turn(cross + left, 1)
    )
    tend = -(u * ((right - left) * 0.5) + v * ((south - north) * 0.5)) - mixing * smooth
    if item // 2 == 2:
        tend = tend + coriolis * v
    if item // 2 == 3:
        tend = tend - coriolis * u
    N[item, begin : begin + count] = (mid + time_step * tend) * wet
    lane = lanes((2, 128))
    for row in (TOP - 1, TOP + TILE - 1):
        swapped = jnp.concatenate([D[item, row + 1 : row + 2], D[item, row : row + 1]], 0)
        diagonal = jnp.where(
            (lane == 0) | (lane == TILE),
            turn(swapped, 1),
            jnp.where((lane == 127) | (lane == TILE - 1), turn(swapped, -1), 0.0),
        )
        N[item, row : row + 2] += (2.0 * time_step * mixing) * diagonal * D[WET, row : row + 2]


def tropic(heights, norths, wet_at, eta, zonal, meridional, begin, count):
    for _ in range(SUBCYCLES):
        heights[begin : begin + count] = eta
        norths[begin : begin + count] = meridional

        def a(shift):
            return heights[begin + shift : begin + shift + count]

        def c(shift):
            return norths[begin + shift : begin + shift + count]

        new_u = zonal - (gravity_step * 0.5) * (turn(eta, -1) - turn(eta, 1))
        new_v = meridional - (gravity_step * 0.5) * (a(1) - a(-1))
        along = (c(1) - c(-1)) - (gravity_step * 0.5) * ((a(2) - eta) - (eta - a(-2)))
        spread = (turn(new_u, -1) - turn(new_u, 1)) + along
        wet = wet_at(begin, count)
        eta = (eta - (depth_step * 0.5) * spread) * wet
        zonal, meridional = new_u * wet, new_v * wet
    return eta, zonal, meridional


def kernel(
    columns,
    near,
    state,
    surface,
    wet,
    new_state,
    new_surface,
    D,
    N,
    heights,
    norths,
    ns,
    sides,
    own_in,
    side_in,
    lists,
    out,
    got,
    eb,
    wb,
    sent,
    came,
):
    column, me = lax.axis_index("tiles"), lax.axis_index("sub")
    half, odd = me // 2, lax.rem(me, 2)
    after, before = lax.rem(column + 1, columns), lax.rem(column + columns - 1, columns)
    source = lax.rem(column + columns + 1 - 2 * odd, columns)
    others = [lax.rem(me + k, SUB) for k in (4, 3, 5, 2, 6, 1, 7)]
    quarters = [lax.rem(half + k, 4) for k in (2, 1, 3, 0)]

    barrier = pltpu.get_barrier_semaphore()
    for r in others:
        pl.semaphore_signal(barrier, inc=1, device_id=(column, r), device_id_type=MESH)
    for k in range(SUB):
        pl.semaphore_signal(barrier, inc=1, device_id=(source, lax.rem(me + k, SUB)), device_id_type=MESH)

    row = lax.broadcasted_iota(jnp.int32, (8, 128), 0)
    mine = jnp.full((8, 128), -1, jnp.int32)
    for direction, base in enumerate((column, column + 1, column, column - 1)):
        listed = near[0, direction]
        slot = jnp.where(listed >= 0, listed - base * SUB, -1)
        mine = jnp.where(row == direction, slot, mine)
    mine = mine.astype(jnp.float32)
    for m in range(SUB):
        ns[m, 16:24] = mine
    for q in range(4):
        sides[0, q, 16:24] = mine
        sides[1, q, 16:24] = mine

    D[...] = jnp.zeros_like(D)
    ocean = wet[...]
    D[WET, TOP : TOP + TILE, 0:TILE] = ocean
    D[ETA, TOP : TOP + TILE, 0:TILE] = surface[...] * ocean
    for item in range(8):
        D[item, TOP : TOP + TILE, 0:TILE] = state[item] * ocean
    pack(D, ns, sides)
    own_in[me] = ns[me]

    def send(source_ref, target, kind, device):
        pltpu.make_async_remote_copy(
            src_ref=source_ref,
            dst_ref=target,
            send_sem=sent.at[kind],
            recv_sem=came.at[kind],
            device_id=device,
            device_id_type=MESH,
        ).start()

    def wait(ref, semaphore):
        pltpu.make_async_copy(ref, ref, semaphore).wait()

    pl.semaphore_wait(barrier, 15)
    for q in quarters:
        send(sides.at[0, q], side_in.at[me], 1, (after, 2 * q + 1))
        send(sides.at[1, q], side_in.at[me], 1, (before, 2 * q))
    for r in others:
        send(ns.at[r], own_in.at[me], 0, (column, r))

    seven, eight = pl.ds(0, SUB - 1), pl.ds(0, SUB)
    wait(own_in.at[seven], came.at[0])
    wait(side_in.at[eight], came.at[1])
    wanted(own_in, side_in, me, lists)

    def picked(which, r, held):
        want = jnp.broadcast_to(lists[which, pl.ds(r, 1)], (8, 128))
        parts = [jnp.zeros((8, 128), jnp.float32)] * 2
        for k in range(SUB):
            hit = want == k
            parts = [jnp.where(hit, held[k, 8 * i : 8 * i + 8], parts[i]) for i in range(2)]
        return parts

    def fill(target, r):
        for which, held in enumerate((own_in, side_in, side_in)):
            for i, part in enumerate(picked(which, r, held)):
                target[r, 16 * which + 8 * i : 16 * which + 8 * i + 8] = part

    for r in others:
        fill(out, r)
        send(out.at[r], got.at[me], 2, (column, r))
    fill(got, me)
    wait(got.at[seven], came.at[2])

    unpack(D, got, eb, wb)
    N[...] = jnp.zeros_like(N)
    heights[...] = jnp.zeros_like(heights)
    norths[...] = jnp.zeros_like(norths)
    weights = (2.0 / 6.0, 4.0 / 6.0)
    fields, other = D, N
    wet_at = lambda begin, count: D[WET, begin : begin + count]
    for step in range(STEPS):
        begin, count = ((8, 96), (16, 80))[step]
        tracer = ((16, 72), (24, 64))[step]
        for item in range(4):
            clinic(fields, other, item, *tracer)
        for item in range(4, 8):
            clinic(fields, other, item, begin, count)
        rows = slice(begin, begin + count)
        old_u = weights[0] * other[4, rows] + weights[1] * other[5, rows]
        old_v = weights[0] * other[6, rows] + weights[1] * other[7, rows]
        eta, zonal, meridional = tropic(heights, norths, wet_at, fields[ETA, rows], old_u, old_v, begin, count)
        other[ETA, rows] = eta
        other[WET] = fields[WET]
        for level in range(2):
            other[4 + level, rows] += zonal - old_u
            other[6 + level, rows] += meridional - old_v
        fields, other = other, fields

    for item in range(8):
        new_state[item] = fields[item, TOP : TOP + TILE, 0:TILE]
    new_surface[...] = fields[ETA, TOP : TOP + TILE, 0:TILE]

    wait(own_in.at[seven], sent.at[0])
    wait(side_in.at[eight], sent.at[1])
    wait(got.at[seven], sent.at[2])


def shards(columns, state, surface, land_mask, neighbours):
    wet = land_mask.reshape(TILE, TILE).astype(jnp.float32)
    vmem = pl.BlockSpec(memory_space=pltpu.VMEM)
    f32 = lambda *shape: pltpu.VMEM(shape, jnp.float32)
    new_state, new_surface = pl.pallas_call(
        functools.partial(kernel, columns),
        out_shape=(
            jax.ShapeDtypeStruct((8, TILE, TILE), jnp.float32),
            jax.ShapeDtypeStruct((TILE, TILE), jnp.float32),
        ),
        in_specs=[pl.BlockSpec(memory_space=pltpu.SMEM), vmem, vmem, vmem],
        out_specs=(vmem, vmem),
        scratch_shapes=[
            f32(10, ROWS, 128),
            f32(10, ROWS, 128),
            f32(ROWS, 128),
            f32(ROWS, 128),
            f32(SUB, 24, 128),
            f32(2, 4, 24, 128),
            f32(SUB, 24, 128),
            f32(SUB, 24, 128),
            f32(3, 8, 128),
            f32(SUB, 48, 128),
            f32(SUB, 48, 128),
            f32(ROWS, 128),
            f32(ROWS, 128),
            pltpu.SemaphoreType.DMA((3,)),
            pltpu.SemaphoreType.DMA((3,)),
        ],
        compiler_params=pltpu.CompilerParams(
            collective_id=0, has_side_effects=True, vmem_limit_bytes=32 * 1024 * 1024
        ),
    )(neighbours, state.reshape(8, TILE, TILE), surface.reshape(TILE, TILE), wet)
    return new_state.reshape(1, 4, 2, TILE * TILE), new_surface.reshape(1, TILE * TILE)


def solution(mesh):
    spec = P(("tiles", "sub"))
    return jax.shard_map(
        functools.partial(shards, mesh.shape["tiles"]),
        mesh=mesh,
        in_specs=(spec, spec, spec, spec),
        out_specs=(spec, spec),
        check_vma=False,
    )
```

time: 46.5 us -> 42.6 us (0.916)
  the two profiles are of different devices: /device:TPU:1 before, /device:TPU:16 now
where the time goes in v2:
time: 42.6 us; the launch traced here: 42.3 us
  Pallas kernels  37.6 us (88%)
  local copies, waits for them, and re-layouts  2.48 us (6%)
  other arithmetic  1.54 us (4%)
  between operations  0.69 us (2%)
    pallas_call x1, Pallas kernels, shards(): pl.pallas_call(functools.partial(kernel, columns), out_shape=(jax.ShapeDt...  37.6 us
    reshape x1, local copies, waits for them, and re-layouts, shards(): new_state.reshape(1, 4, 2, TILE * TILE)  0.92 us

profile of v2, /device:TPU:16, one launch (start us, length us, event | category | flops | bytes accessed | tf_op | source)
XLA Modules:
  0.0 42.3 jit_solution(9925485495560002856)
XLA Ops:
  0.6 0.0 copy-start.1
  0.6 0.8 %reduce = f32[3600]{0:T(1024)S(1)} reduce(f32[1,3600]{1,0:T(1,128)} %param.5, f32[]{:T(128)} %constant.4), dimensions={0}, to_apply=%param.5.reduce_sub_computation | reduce | bytes 28804 | tf_op args[1]
  1.4 0.1 reshape.19.surface
  1.5 0.8 %convert_reduce_fusion = f32[3600]{0:T(1024)S(1)} fusion(s32[1,3600]{1,0:T(1,128)} %param.6), kind=kLoop, calls=%fused_computation | loop fusion | flops 3600 | bytes 28800 | tf_op jit(solution)/shard_map/convert_element_type | solution.py:314
  2.3 0.1 convert_element_type.6.wet
  2.4 0.0 copy-done.1
  2.4 0.0 copy-start
  2.4 0.4 reshape.18.state
  2.8 0.3 copy-done
  3.1 37.6 %shard_map.59 = (f32[8,60,60]{2,1,0:T(8,128)S(1)}, f32[60,60]{1,0:T(8,128)S(1)}) custom-call(s32[1,4]{1,0:T(1,128)S(1)} %copy-done, f32[8,60,60]{2,1,0:T(8,128)S(1)} %reshape.18.state, f32[60,60]{1,0:T(8,128)S(1)} %reshape.19.surface, f32[60,60]{1,0:T(8,128)S(1)} %convert_element_type.6.wet), custom_call_target="tpu_custom_call" | custom-call | tf_op jit(solution)/shard_map/pallas_call | solution.py:317
  40.7 0.9 %reshape.20 = f32[1,4,2,3600]{3,2,1,0:T(2,128)} reshape(f32[8,60,60]{2,1,0:T(8,128)S(1)} %get-tuple-element.4) | data formatting | bytes 230400 | tf_op jit(solution)/shard_map/reshape | solution.py:346
  41.6 0.7 %reshape.21 = f32[1,3600]{1,0:T(1,128)} reshape(f32[60,60]{1,0:T(8,128)S(1)} %get-tuple-element.5) | data formatting | bytes 28800 | tf_op jit(solution)/shard_map/reshape | solution.py:346
Async XLA Ops:
  0.6 1.8 %copy-start.1 = (f32[1,4,2,3600]{3,2,1,0:T(2,128)S(1)}, f32[1,4,2,3600]{3,2,1,0:T(2,128)}, u32[]{:S(2)}) copy-start(f32[1,4,2,3600]{3,2,1,0:T(2,128)} %param.4) | copy-start | bytes 345604
  2.4 0.7 %copy-start = (s32[1,4]{1,0:T(1,128)S(1)}, s32[1,4]{1,0:T(1,128)}, u32[]{:S(2)}) copy-start(s32[1,4]{1,0:T(1,128)} %near.1) | copy-start | bytes 52

commit v3 on v2

--- a/solution.py
+++ b/solution.py
@@ -28,6 +28,7 @@
     + [(i, 100 + 4 * i, 4) for i in range(4)]
 )
 QUARTERS = (0, 16, 28, 44)
+LISTED = 116
 
 
 def lanes(shape):
@@ -41,6 +42,38 @@
 
 def within(lane, first, count):
     return (lane >= first) & (lane < first + count)
+
+
+def spread(tile_of, last, write):
+    lane = lanes((8, 128))
+    for b in range(8):
+        row = 8 * b + lax.broadcasted_iota(jnp.int32, (8, 128), 0)
+        begin = TILE * row
+        tile = (begin + ((lane - begin) & 127)) >> 7
+        first = (480 * b) // 128
+        flat = jnp.zeros((8, 128), jnp.float32)
+        for a in range(first, min((480 * b + 479) // 128, 28) + 1):
+            flat = jnp.where(tile == a, jnp.broadcast_to(last if a == 28 else tile_of(a), (8, 128)), flat)
+        flat = jnp.where(row & 1 == 1, turn(flat, 64), flat)
+        rows = pltpu.roll(flat, (-480 * b) % 128, 1, stride=4, stride_axis=0)
+        count = min(8, TILE - 8 * b)
+        write(8 * b, count, jnp.where(lane < TILE, rows, 0.0)[0:count])
+
+
+def flatten(rows, b):
+    row = lax.broadcasted_iota(jnp.int32, (8, 128), 0)
+    rows = jnp.where(row & 1 == 1, turn(rows, 480 * b + 60), turn(rows, 480 * b))
+    rows = jnp.where(row & 2 == 2, turn(rows, 120), rows)
+    return jnp.where(row & 4 == 4, turn(rows, 240), rows)
+
+
+def joined(row_of, a, height):
+    lane = lanes((height, 128)) + 128 * a
+    first = (128 * a) // TILE
+    out = row_of(first)
+    for i in range(first + 1, min((128 * a + 127) // TILE, TILE - 1) + 1):
+        out = jnp.where(lane < TILE * i, out, row_of(i))
+    return out
 
 
 def pack(D, ns, sides):
@@ -74,13 +107,17 @@
 
 
 def wanted(own_in, side_in, me, lists):
-    def column(held, direction):
-        return jnp.concatenate([held[r, 16 + direction : 17 + direction] for r in range(SUB)], 0)
-
-    north, east, south, west = (column(own_in, direction) for direction in range(4))
+    def table(held):
+        return jnp.concatenate([held[r, 0:1] for r in range(SUB)], 0)
+
+    def column(rows, lane):
+        return jnp.broadcast_to(rows[:, lane : lane + 1], (SUB, 128))
+
+    own, side = table(own_in), table(side_in)
+    north, east, south, west = (column(own, TILE + direction) for direction in range(4))
     beside = jnp.where(lax.rem(me, 2) == 0, east, west)
-    up = jnp.where(north >= 0, take(beside, north), take(column(side_in, 0), beside))
-    down = jnp.where(south >= 0, take(beside, south), take(column(side_in, 2), beside))
+    up = jnp.where(north >= 0, take(beside, north), take(column(side, LISTED), beside))
+    down = jnp.where(south >= 0, take(beside, south), take(column(side, LISTED + 2), beside))
     lists[0] = jnp.where(lanes((SUB, 128)) < 64, south, north)
     lists[1] = beside
     lists[2] = jnp.where(me >= 4, up, down)
@@ -175,12 +212,19 @@
 
 def kernel(
     columns,
-    near,
+    near_in,
+    state_in,
+    surface_in,
+    mask_in,
+    new_state,
+    new_surface,
     state,
     surface,
-    wet,
-    new_state,
-    new_surface,
+    mask,
+    tails,
+    turned,
+    near,
+    loaded,
     D,
     N,
     heights,
@@ -205,31 +249,58 @@
     quarters = [lax.rem(half + k, 4) for k in (2, 1, 3, 0)]
 
     barrier = pltpu.get_barrier_semaphore()
-    for r in others:
-        pl.semaphore_signal(barrier, inc=1, device_id=(column, r), device_id_type=MESH)
-    for k in range(SUB):
-        pl.semaphore_signal(barrier, inc=1, device_id=(source, lax.rem(me + k, SUB)), device_id_type=MESH)
-
-    row = lax.broadcasted_iota(jnp.int32, (8, 128), 0)
-    mine = jnp.full((8, 128), -1, jnp.int32)
+    for k in (4, 3, 5, 2, 6, 1, 7, 0):
+        r = lax.rem(me + k, SUB)
+        pl.semaphore_signal(barrier, inc=1, device_id=(source, r), device_id_type=MESH)
+        if k:
+            pl.semaphore_signal(barrier, inc=1, device_id=(column, r), device_id_type=MESH)
+
+    loads = [
+        pltpu.make_async_copy(held, target, loaded.at[i])
+        for i, (held, target) in enumerate(((mask_in, mask), (surface_in, surface), (state_in, state), (near_in, near)))
+    ]
+    for load in loads:
+        load.start()
+    D[...] = jnp.zeros_like(D)
+
+    def put(item):
+        def write(at, count, rows):
+            if item != WET:
+                rows = rows * D[WET, TOP + at : TOP + at + count]
+            D[item, TOP + at : TOP + at + count] = rows
+
+        return write
+
+    loads[0].wait()
+    tails[0:1, 0:16] = mask[0:1, 3584:3600].astype(jnp.float32)
+    spread(lambda a: mask[0:1, 128 * a : 128 * a + 128].astype(jnp.float32), tails[0:1], put(WET))
+    loads[1].wait()
+    tails[1:2, 0:16] = surface[0:1, 3584:3600]
+    spread(lambda a: surface[0:1, 128 * a : 128 * a + 128], tails[1:2], put(ETA))
+    loads[2].wait()
+    for field in range(4):
+        tails[8 + 2 * field : 10 + 2 * field, 0:16] = state[0, field, :, 3584:3600]
+        for level in range(2):
+            item = 2 * field + level
+            spread(
+                lambda a, field=field, level=level: state[0, field, level : level + 1, 128 * a : 128 * a + 128],
+                tails[8 + item : 9 + item],
+                put(item),
+            )
+    pack(D, ns, sides)
+    loads[3].wait()
+    lane = lanes((1, 128))
+    mine = jnp.zeros((1, 128), jnp.float32)
     for direction, base in enumerate((column, column + 1, column, column - 1)):
         listed = near[0, direction]
-        slot = jnp.where(listed >= 0, listed - base * SUB, -1)
-        mine = jnp.where(row == direction, slot, mine)
-    mine = mine.astype(jnp.float32)
+        slot = jnp.where(listed >= 0, listed - base * SUB, -1).astype(jnp.float32)
+        mine = jnp.where(lane == TILE + direction, slot, mine)
     for m in range(SUB):
-        ns[m, 16:24] = mine
+        ns[m, 0:1] += mine
+    mine = turn(mine, LISTED - TILE)
     for q in range(4):
-        sides[0, q, 16:24] = mine
-        sides[1, q, 16:24] = mine
-
-    D[...] = jnp.zeros_like(D)
-    ocean = wet[...]
-    D[WET, TOP : TOP + TILE, 0:TILE] = ocean
-    D[ETA, TOP : TOP + TILE, 0:TILE] = surface[...] * ocean
-    for item in range(8):
-        D[item, TOP : TOP + TILE, 0:TILE] = state[item] * ocean
-    pack(D, ns, sides)
+        sides[0, q, 0:1] += mine
+        sides[1, q, 0:1] += mine
     own_in[me] = ns[me]
 
     def send(source_ref, target, kind, device):
@@ -265,16 +336,25 @@
             parts = [jnp.where(hit, held[k, 8 * i : 8 * i + 8], parts[i]) for i in range(2)]
         return parts
 
-    def fill(target, r):
-        for which, held in enumerate((own_in, side_in, side_in)):
+    outer = (half == 0) | (half == 3)
+    first = lambda count, rows: got.at[pl.ds(0, count), pl.ds(0, rows)]
+
+    def fill(target, r, pieces):
+        for which, held in enumerate((own_in, side_in, side_in)[:pieces]):
             for i, part in enumerate(picked(which, r, held)):
                 target[r, 16 * which + 8 * i : 16 * which + 8 * i + 8] = part
 
-    for r in others:
-        fill(out, r)
-        send(out.at[r], got.at[me], 2, (column, r))
-    fill(got, me)
-    wait(got.at[seven], came.at[2])
+    def second_hop(kind, pieces):
+        rows = pl.ds(0, 16 * pieces)
+        for r in others:
+            fill(out, r, pieces)
+            send(out.at[r, rows], got.at[me, rows], kind, (column, r))
+        fill(got, me, pieces)
+        wait(first(4 - (kind == 2), 48), came.at[2])
+        wait(first(4 - (kind == 3), 32), came.at[3])
+
+    pl.when(outer)(lambda: second_hop(2, 3))
+    pl.when(jnp.logical_not(outer))(lambda: second_hop(3, 2))
 
     unpack(D, got, eb, wb)
     N[...] = jnp.zeros_like(N)
@@ -303,47 +383,59 @@
 
     for item in range(8):
         new_state[item] = fields[item, TOP : TOP + TILE, 0:TILE]
-    new_surface[...] = fields[ETA, TOP : TOP + TILE, 0:TILE]
+    for b in range(8):
+        turned[8 * b : 8 * b + 8] = flatten(fields[ETA, TOP + 8 * b : TOP + 8 * b + 8], b)
+    for a in range(29):
+        width = min(128, TILE * TILE - 128 * a)
+        tile = joined(lambda i: turned[i : i + 1], a, 1)
+        new_surface[0:1, 128 * a : 128 * a + width] = tile[:, 0:width]
 
     wait(own_in.at[seven], sent.at[0])
     wait(side_in.at[eight], sent.at[1])
-    wait(got.at[seven], sent.at[2])
+    pl.when(outer)(lambda: wait(first(7, 48), sent.at[2]))
+    pl.when(jnp.logical_not(outer))(lambda: wait(first(7, 32), sent.at[3]))
 
 
 def shards(columns, state, surface, land_mask, neighbours):
-    wet = land_mask.reshape(TILE, TILE).astype(jnp.float32)
-    vmem = pl.BlockSpec(memory_space=pltpu.VMEM)
+    hbm, vmem = pl.BlockSpec(memory_space=pltpu.HBM), pl.BlockSpec(memory_space=pltpu.VMEM)
     f32 = lambda *shape: pltpu.VMEM(shape, jnp.float32)
     new_state, new_surface = pl.pallas_call(
         functools.partial(kernel, columns),
         out_shape=(
             jax.ShapeDtypeStruct((8, TILE, TILE), jnp.float32),
-            jax.ShapeDtypeStruct((TILE, TILE), jnp.float32),
+            jax.ShapeDtypeStruct(surface.shape, jnp.float32),
         ),
-        in_specs=[pl.BlockSpec(memory_space=pltpu.SMEM), vmem, vmem, vmem],
+        in_specs=[hbm] * 4,
         out_specs=(vmem, vmem),
         scratch_shapes=[
+            f32(*state.shape),
+            f32(*surface.shape),
+            pltpu.VMEM(surface.shape, jnp.int32),
+            f32(16, 128),
+            f32(64, 128),
+            pltpu.SMEM((1, 4), jnp.int32),
+            pltpu.SemaphoreType.DMA((4,)),
             f32(10, ROWS, 128),
             f32(10, ROWS, 128),
             f32(ROWS, 128),
             f32(ROWS, 128),
-            f32(SUB, 24, 128),
-            f32(2, 4, 24, 128),
-            f32(SUB, 24, 128),
-            f32(SUB, 24, 128),
+            f32(SUB, 16, 128),
+            f32(2, 4, 16, 128),
+            f32(SUB, 16, 128),
+            f32(SUB, 16, 128),
             f32(3, 8, 128),
             f32(SUB, 48, 128),
             f32(SUB, 48, 128),
             f32(ROWS, 128),
             f32(ROWS, 128),
-            pltpu.SemaphoreType.DMA((3,)),
-            pltpu.SemaphoreType.DMA((3,)),
+            pltpu.SemaphoreType.DMA((4,)),
+            pltpu.SemaphoreType.DMA((4,)),
         ],
         compiler_params=pltpu.CompilerParams(
-            collective_id=0, has_side_effects=True, vmem_limit_bytes=32 * 1024 * 1024
+            collective_id=0, has_side_effects=True, vmem_limit_bytes=56 * 1024 * 1024
         ),
-    )(neighbours, state.reshape(8, TILE, TILE), surface.reshape(TILE, TILE), wet)
-    return new_state.reshape(1, 4, 2, TILE * TILE), new_surface.reshape(1, TILE * TILE)
+    )(neighbours, state, surface, land_mask)
+    return new_state.reshape(state.shape), new_surface
 
 
 def solution(mesh):

time: 42.6 us -> 40.4 us (0.948)
  other arithmetic: 1.54 us -> 0 us
  Pallas kernels: 37.6 us -> 37.1 us
    unnamed x1 -> x0, other arithmetic: 0.79 us -> none
    convert_element_type x1 -> x0, other arithmetic: 0.76 us -> none  [shards(): wet = land_mask.reshape(TILE, TILE).astype(jnp.float32)]
    pallas_call x1, Pallas kernels: 37.6 us -> 37.1 us  [shards(): pl.pallas_call(functools.partial(kernel, columns), out_shape=(jax.ShapeDt...]
    reshape x4 -> x1, local copies, waits for them, and re-layouts: 2.11 us -> 1.87 us  [shards(): return (new_state.reshape(state.shape), new_surface)]
where the time goes in v3:
time: 40.4 us; the launch traced here: 40.2 us
  Pallas kernels  37.1 us (92%)
  local copies, waits for them, and re-layouts  2.47 us (6%)
  between operations  0.65 us (2%)
    pallas_call x1, Pallas kernels, shards(): pl.pallas_call(functools.partial(kernel, columns), out_shape=(jax.ShapeDt...  37.1 us
    reshape x1, local copies, waits for them, and re-layouts, shards(): return (new_state.reshape(state.shape), new_surface)  1.87 us

profile of v3, /device:TPU:16, one launch (start us, length us, event | category | flops | bytes accessed | tf_op | source)
XLA Modules:
  0.0 40.2 jit_solution(3324097540894929641)
XLA Ops:
  0.6 37.1 %shard_map.59 = (f32[8,60,60]{2,1,0:T(8,128)}, f32[1,3600]{1,0:T(1,128)}) custom-call(s32[1,4]{1,0:T(1,128)} %near_in.1, f32[1,4,2,3600]{3,2,1,0:T(2,128)} %state_in.1, f32[1,3600]{1,0:T(1,128)} %surface_in.1, s32[1,3600]{1,0:T(1,128)} %mask_in.1), custom_call_target="tpu_custom_call" | custom-call | tf_op jit(solution)/shard_map/pallas_call | solution.py:402
  37.8 0.0 copy-start
  37.8 1.9 %reshape.7 = f32[1,4,2,3600]{3,2,1,0:T(2,128)} reshape(f32[8,60,60]{2,1,0:T(8,128)} %get-tuple-element.4) | data formatting | bytes 230400 | tf_op jit(solution)/shard_map/reshape | solution.py:438
  39.6 0.0 copy-done
  39.6 0.6 %copy.7 = f32[1,3600]{1,0:T(1,128)} copy(f32[1,3600]{1,0:T(1,128)S(1)} %copy-done) | data formatting | bytes 28800
Async XLA Ops:
  37.8 1.9 %copy-start = (f32[1,3600]{1,0:T(1,128)S(1)}, f32[1,3600]{1,0:T(1,128)}, u32[]{:S(2)}) copy-start(f32[1,3600]{1,0:T(1,128)} %get-tuple-element.9) | copy-start | bytes 43204

commit v4 on v3

--- a/solution.py
+++ b/solution.py
@@ -27,7 +27,7 @@
     + [(ETA, 68, 16), (WET, 84, 16)]
     + [(i, 100 + 4 * i, 4) for i in range(4)]
 )
-QUARTERS = (0, 16, 28, 44)
+HALVES = (0, 28)
 LISTED = 116
 
 
@@ -81,12 +81,12 @@
         return D[item, TOP + north : TOP + north + count] + turn(D[item, TOP + south : TOP + south + count], 64)
 
     for i in range(4):
-        ns[i, 0:16] = both(4 + i, 0, 43, 16)
-        ns[6, 4 * i : 4 * i + 4] = both(i, 0, 56, 4)
-        ns[7, i : i + 1] = both(4 + i, 16, 59, 1)
-    ns[4, 0:16] = both(ETA, 0, 44, 16)
-    ns[5, 0:16] = both(WET, 0, 44, 16)
-    ns[7, 4:16] = jnp.zeros((12, 128), jnp.float32)
+        ns[i // 2, 16 * (i % 2) : 16 * (i % 2) + 16] = both(4 + i, 0, 43, 16)
+        ns[3, 4 * i : 4 * i + 4] = both(i, 0, 56, 4)
+        ns[3, 16 + i : 17 + i] = both(4 + i, 16, 59, 1)
+    ns[2, 0:16] = both(ETA, 0, 44, 16)
+    ns[2, 16:32] = both(WET, 0, 44, 16)
+    ns[3, 20:32] = jnp.zeros((12, 128), jnp.float32)
     lane = lanes((TILE, 128))
     east = west = jnp.zeros((TILE, 128), jnp.float32)
     for item, first, depth in ITEMS:
@@ -94,9 +94,9 @@
         here = within(lane, first, depth)
         east = jnp.where(here, turn(whole, first - (TILE - depth)), east)
         west = jnp.where(here, turn(whole, first), west)
-    for q, row in enumerate(QUARTERS):
-        sides[0, q, 0:16] = east[row : row + 16]
-        sides[1, q, 0:16] = west[row : row + 16]
+    for half, row in enumerate(HALVES):
+        sides[0, half] = east[row : row + 32]
+        sides[1, half] = west[row : row + 32]
 
 
 def take(table, index):
@@ -106,30 +106,32 @@
     return out
 
 
-def wanted(own_in, side_in, me, lists):
-    def table(held):
-        return jnp.concatenate([held[r, 0:1] for r in range(SUB)], 0)
-
-    def column(rows, lane):
-        return jnp.broadcast_to(rows[:, lane : lane + 1], (SUB, 128))
-
-    own, side = table(own_in), table(side_in)
-    north, east, south, west = (column(own, TILE + direction) for direction in range(4))
+def table(held):
+    return jnp.concatenate([held[r, 0:1] for r in range(SUB)], 0)
+
+
+def column_of(rows, lane):
+    return jnp.broadcast_to(rows[:, lane : lane + 1], (SUB, 128))
+
+
+def wanted(own_in, me, lists):
+    own = table(own_in)
+    north, east, south, west = (column_of(own, TILE + direction) for direction in range(4))
     beside = jnp.where(lax.rem(me, 2) == 0, east, west)
-    up = jnp.where(north >= 0, take(beside, north), take(column(side, LISTED), beside))
-    down = jnp.where(south >= 0, take(beside, south), take(column(side, LISTED + 2), beside))
     lists[0] = jnp.where(lanes((SUB, 128)) < 64, south, north)
     lists[1] = beside
-    lists[2] = jnp.where(me >= 4, up, down)
-
-
-def unpack(D, got, eb, wb):
-    for held, odd in ((eb, 0), (wb, 1)):
-        held[8:24] = got[6 + odd, 32:48]
-        for q, row in enumerate(QUARTERS):
-            held[TOP + row : TOP + row + 16] = got[2 * q + odd, 16:32]
-        held[84:100] = got[odd, 32:48]
-
+    beyond = jnp.where(lax.rem(me, 4) >= 2, north, south)
+    lists[3] = beyond
+    lists[4] = take(beside, beyond)
+
+
+def corners(side_in, me, lists):
+    side = table(side_in)
+    around = jnp.where(lax.rem(me, 4) >= 2, column_of(side, LISTED), column_of(side, LISTED + 2))
+    lists[2] = jnp.where(lists[3] >= 0, lists[4], take(around, lists[1]))
+
+
+def unpack_ends(D, got):
     def put(item, rows, north, south):
         count = rows.shape[0]
         tile = lanes((count, 128)) < TILE
@@ -137,11 +139,19 @@
         D[item, TOP + south : TOP + south + count] = jnp.where(tile, rows, 0.0)
 
     for i in range(4):
-        put(4 + i, got[i, 0:16], -17, 60)
-        put(4 + i, got[7, i : i + 1], -1, 76)
-        put(i, got[6, 4 * i : 4 * i + 4], -4, 60)
-    put(ETA, got[4, 0:16], -16, 60)
-    put(WET, got[5, 0:16], -16, 60)
+        put(4 + i, got[i // 2, 16 * (i % 2) : 16 * (i % 2) + 16], -17, 60)
+        put(4 + i, got[3, 16 + i : 17 + i], -1, 76)
+        put(i, got[3, 4 * i : 4 * i + 4], -4, 60)
+    put(ETA, got[2, 0:16], -16, 60)
+    put(WET, got[2, 16:32], -16, 60)
+
+
+def unpack_sides(D, got, eb, wb):
+    for held, odd in ((eb, 0), (wb, 1)):
+        held[8:24] = got[2 + odd, 64:80]
+        for half, row in enumerate(HALVES):
+            held[TOP + row : TOP + row + 32] = got[2 * half + odd, 32:64]
+        held[84:100] = got[odd, 64:80]
 
     for item, first, depth in ITEMS:
         beyond = min(depth, 16)
@@ -153,31 +163,27 @@
         D[item, begin : begin + count] = D[item, begin : begin + count] + sides
 
 
-def clinic(D, N, item, begin, count):
+def clinic(D, N, wets, item, begin, count):
     level = item % 2
 
     def at(which, shift=0):
         return D[which, begin + shift : begin + shift + count]
 
     mid, north, south = at(item), at(item, -1), at(item, 1)
-    wet = at(WET)
-    u, v = at(4 + level), at(6 + level)
+    half_u = (0.5 * time_step) * at(4 + level)
+    half_v = (0.5 * time_step) * at(6 + level)
     right, left = turn(mid, -1), turn(mid, 1)
-    cross = 2.0 * (north + south) - 8.0 * mid
-    smooth = (
-        20.0 * mid
-        - 8.0 * (north + south)
-        + at(item, -2)
-        + at(item, 2)
-        + turn(cross + right, -1)
-        + turn(cross + left, 1)
-    )
-    tend = -(u * ((right - left) * 0.5) + v * ((south - north) * 0.5)) - mixing * smooth
+    pair = north + south
+    cross = 2.0 * pair - 8.0 * mid
+    far = (at(item, -2) + at(item, 2)) + (turn(cross + right, -1) + turn(cross + left, 1))
+    rate = time_step * mixing
+    new = (1.0 - 20.0 * rate) * mid + (8.0 * rate) * pair - rate * far
+    new = new - half_u * (right - left) - half_v * (south - north)
     if item // 2 == 2:
-        tend = tend + coriolis * v
+        new = new + (2.0 * coriolis) * half_v
     if item // 2 == 3:
-        tend = tend - coriolis * u
-    N[item, begin : begin + count] = (mid + time_step * tend) * wet
+        new = new - (2.0 * coriolis) * half_u
+    N[item, begin : begin + count] = new * wets[begin : begin + count]
     lane = lanes((2, 128))
     for row in (TOP - 1, TOP + TILE - 1):
         swapped = jnp.concatenate([D[item, row + 1 : row + 2], D[item, row : row + 1]], 0)
@@ -186,7 +192,7 @@
             turn(swapped, 1),
             jnp.where((lane == 127) | (lane == TILE - 1), turn(swapped, -1), 0.0),
         )
-        N[item, row : row + 2] += (2.0 * time_step * mixing) * diagonal * D[WET, row : row + 2]
+        N[item, row : row + 2] += (2.0 * rate) * diagonal * wets[row : row + 2]
 
 
 def tropic(heights, norths, wet_at, eta, zonal, meridional, begin, count):
@@ -242,11 +248,13 @@
     came,
 ):
     column, me = lax.axis_index("tiles"), lax.axis_index("sub")
-    half, odd = me // 2, lax.rem(me, 2)
+    quarter, odd = lax.rem(me, 4), lax.rem(me, 2)
     after, before = lax.rem(column + 1, columns), lax.rem(column + columns - 1, columns)
     source = lax.rem(column + columns + 1 - 2 * odd, columns)
     others = [lax.rem(me + k, SUB) for k in (4, 3, 5, 2, 6, 1, 7)]
-    quarters = [lax.rem(half + k, 4) for k in (2, 1, 3, 0)]
+    pairs = [lax.rem(me // 2 + k, 4) for k in (2, 1, 3, 0)]
+    turns = 1 - 2 * lax.rem(column, 2)
+    close = [lax.rem(me + SUB + turns * k, SUB) for k in (2, 1, -1)]
 
     barrier = pltpu.get_barrier_semaphore()
     for k in (4, 3, 5, 2, 6, 1, 7, 0):
@@ -295,13 +303,13 @@
         listed = near[0, direction]
         slot = jnp.where(listed >= 0, listed - base * SUB, -1).astype(jnp.float32)
         mine = jnp.where(lane == TILE + direction, slot, mine)
-    for m in range(SUB):
-        ns[m, 0:1] += mine
+    for q in range(4):
+        ns[q, 0:1] += mine
     mine = turn(mine, LISTED - TILE)
-    for q in range(4):
-        sides[0, q, 0:1] += mine
-        sides[1, q, 0:1] += mine
-    own_in[me] = ns[me]
+    for half in range(2):
+        sides[0, half, 0:1] += mine
+        sides[1, half, 0:1] += mine
+    own_in[me] = ns[quarter]
 
     def send(source_ref, target, kind, device):
         pltpu.make_async_remote_copy(
@@ -317,49 +325,51 @@
         pltpu.make_async_copy(ref, ref, semaphore).wait()
 
     pl.semaphore_wait(barrier, 15)
-    for q in quarters:
-        send(sides.at[0, q], side_in.at[me], 1, (after, 2 * q + 1))
-        send(sides.at[1, q], side_in.at[me], 1, (before, 2 * q))
+    for pair in pairs:
+        half = lax.rem(pair, 2)
+        send(sides.at[0, half], side_in.at[me], 1, (after, 2 * pair + 1))
+        send(sides.at[1, half], side_in.at[me], 1, (before, 2 * pair))
     for r in others:
-        send(ns.at[r], own_in.at[me], 0, (column, r))
-
-    seven, eight = pl.ds(0, SUB - 1), pl.ds(0, SUB)
-    wait(own_in.at[seven], came.at[0])
-    wait(side_in.at[eight], came.at[1])
-    wanted(own_in, side_in, me, lists)
-
-    def picked(which, r, held):
-        want = jnp.broadcast_to(lists[which, pl.ds(r, 1)], (8, 128))
-        parts = [jnp.zeros((8, 128), jnp.float32)] * 2
-        for k in range(SUB):
-            hit = want == k
-            parts = [jnp.where(hit, held[k, 8 * i : 8 * i + 8], parts[i]) for i in range(2)]
-        return parts
-
-    outer = (half == 0) | (half == 3)
-    first = lambda count, rows: got.at[pl.ds(0, count), pl.ds(0, rows)]
-
-    def fill(target, r, pieces):
-        for which, held in enumerate((own_in, side_in, side_in)[:pieces]):
-            for i, part in enumerate(picked(which, r, held)):
-                target[r, 16 * which + 8 * i : 16 * which + 8 * i + 8] = part
-
-    def second_hop(kind, pieces):
-        rows = pl.ds(0, 16 * pieces)
-        for r in others:
-            fill(out, r, pieces)
-            send(out.at[r, rows], got.at[me, rows], kind, (column, r))
-        fill(got, me, pieces)
-        wait(first(4 - (kind == 2), 48), came.at[2])
-        wait(first(4 - (kind == 3), 32), came.at[3])
-
-    pl.when(outer)(lambda: second_hop(2, 3))
-    pl.when(jnp.logical_not(outer))(lambda: second_hop(3, 2))
-
-    unpack(D, got, eb, wb)
+        send(ns.at[lax.rem(r, 4)], own_in.at[me], 0, (column, r))
+
     N[...] = jnp.zeros_like(N)
     heights[...] = jnp.zeros_like(heights)
     norths[...] = jnp.zeros_like(norths)
+
+    def fill(target, slot, r, which, held, begin, at, count):
+        want = jnp.broadcast_to(lists[which, pl.ds(r, 1)], (8, 128))
+        parts = [jnp.zeros((8, 128), jnp.float32)] * (count // 8)
+        for k in range(SUB):
+            hit = want == k
+            for i in range(count // 8):
+                parts[i] = jnp.where(hit, held[k, pl.ds(begin + 8 * i, 8)], parts[i])
+        for i, part in enumerate(parts):
+            target[slot, at + 8 * i : at + 8 * i + 8] = part
+
+    def fill_sides(target, slot, r):
+        fill(target, slot, r, 1, side_in, 0, 32, 32)
+        fill(target, slot, r, 2, side_in, pl.multiple_of(16 * (quarter // 2), 16), 64, 16)
+
+    seven, eight, three = pl.ds(0, SUB - 1), pl.ds(0, SUB), pl.ds(0, 3)
+    ends, flanks = pl.ds(0, 32), pl.ds(32, 48)
+    wait(own_in.at[seven], came.at[0])
+    wanted(own_in, me, lists)
+    for i, r in enumerate(close):
+        fill(out, i, r, 0, own_in, 0, 0, 32)
+        send(out.at[i, ends], got.at[quarter, ends], 2, (column, r))
+    fill(got, quarter, me, 0, own_in, 0, 0, 32)
+
+    wait(side_in.at[eight], came.at[1])
+    corners(side_in, me, lists)
+    for i, r in enumerate(close):
+        fill_sides(out, i, r)
+        send(out.at[i, flanks], got.at[quarter, flanks], 3, (column, r))
+    fill_sides(got, quarter, me)
+
+    wait(got.at[three, ends], came.at[2])
+    unpack_ends(D, got)
+    wait(got.at[three, flanks], came.at[3])
+    unpack_sides(D, got, eb, wb)
     weights = (2.0 / 6.0, 4.0 / 6.0)
     fields, other = D, N
     wet_at = lambda begin, count: D[WET, begin : begin + count]
@@ -367,15 +377,14 @@
         begin, count = ((8, 96), (16, 80))[step]
         tracer = ((16, 72), (24, 64))[step]
         for item in range(4):
-            clinic(fields, other, item, *tracer)
+            clinic(fields, other, D.at[WET], item, *tracer)
         for item in range(4, 8):
-            clinic(fields, other, item, begin, count)
+            clinic(fields, other, D.at[WET], item, begin, count)
         rows = slice(begin, begin + count)
         old_u = weights[0] * other[4, rows] + weights[1] * other[5, rows]
         old_v = weights[0] * other[6, rows] + weights[1] * other[7, rows]
         eta, zonal, meridional = tropic(heights, norths, wet_at, fields[ETA, rows], old_u, old_v, begin, count)
         other[ETA, rows] = eta
-        other[WET] = fields[WET]
         for level in range(2):
             other[4 + level, rows] += zonal - old_u
             other[6 + level, rows] += meridional - old_v
@@ -392,8 +401,8 @@
 
     wait(own_in.at[seven], sent.at[0])
     wait(side_in.at[eight], sent.at[1])
-    pl.when(outer)(lambda: wait(first(7, 48), sent.at[2]))
-    pl.when(jnp.logical_not(outer))(lambda: wait(first(7, 32), sent.at[3]))
+    wait(got.at[three, ends], sent.at[2])
+    wait(got.at[three, flanks], sent.at[3])
 
 
 def shards(columns, state, surface, land_mask, neighbours):
@@ -419,22 +428,22 @@
             f32(10, ROWS, 128),
             f32(ROWS, 128),
             f32(ROWS, 128),
-            f32(SUB, 16, 128),
-            f32(2, 4, 16, 128),
-            f32(SUB, 16, 128),
-            f32(SUB, 16, 128),
-            f32(3, 8, 128),
-            f32(SUB, 48, 128),
-            f32(SUB, 48, 128),
+            f32(4, 32, 128),
+            f32(2, 2, 32, 128),
+            f32(SUB, 32, 128),
+            f32(SUB, 32, 128),
+            f32(5, 8, 128),
+            f32(3, 80, 128),
+            f32(4, 80, 128),
             f32(ROWS, 128),
             f32(ROWS, 128),
             pltpu.SemaphoreType.DMA((4,)),
             pltpu.SemaphoreType.DMA((4,)),
         ],
         compiler_params=pltpu.CompilerParams(
-            collective_id=0, has_side_effects=True, vmem_limit_bytes=56 * 1024 * 1024
+            collective_id=0, has_side_effects=True, vmem_limit_bytes=32 * 1024 * 1024
         ),
-    )(neighbours, state, surface, land_mask)
+    )(*(pltpu.with_memory_space_constraint(x, pltpu.HBM) for x in (neighbours, state, surface, land_mask)))
     return new_state.reshape(state.shape), new_surface
 
 

time: 40.4 us -> 38.5 us (0.953)
  local copies, waits for them, and re-layouts: 2.47 us -> 1.52 us
  Pallas kernels: 37.1 us -> 36.2 us
    reshape x1, local copies, waits for them, and re-layouts: 1.87 us -> 0.92 us  [shards(): return (new_state.reshape(state.shape), new_surface)]
    pallas_call x1, Pallas kernels: 37.1 us -> 36.2 us  [shards(): pl.pallas_call(functools.partial(kernel, columns), out_shape=(jax.ShapeDt...]
where the time goes in v4:
time: 38.5 us; the launch traced here: 38.3 us
  Pallas kernels  36.2 us (94%)
  local copies, waits for them, and re-layouts  1.52 us (4%)
  between operations  0.64 us (2%)
    pallas_call x1, Pallas kernels, shards(): pl.pallas_call(functools.partial(kernel, columns), out_shape=(jax.ShapeDt...  36.2 us
    reshape x1, local copies, waits for them, and re-layouts, shards(): return (new_state.reshape(state.shape), new_surface)  0.92 us

profile of v4, /device:TPU:16, one launch (start us, length us, event | category | flops | bytes accessed | tf_op | source)
XLA Modules:
  0.0 38.3 jit_solution(13611995491992679899)
XLA Ops:
  0.6 36.2 %shard_map.59 = (f32[8,60,60]{2,1,0:T(8,128)S(1)}, f32[1,3600]{1,0:T(1,128)S(1)}) custom-call(s32[1,4]{1,0:T(1,128)} %near_in.1, f32[1,4,2,3600]{3,2,1,0:T(2,128)} %state_in.1, f32[1,3600]{1,0:T(1,128)} %surface_in.1, s32[1,3600]{1,0:T(1,128)} %mask_in.1), custom_call_target="tpu_custom_call" | custom-call | tf_op jit(solution)/shard_map/pallas_call | solution.py:411
  36.8 0.9 %reshape.7 = f32[1,4,2,3600]{3,2,1,0:T(2,128)} reshape(f32[8,60,60]{2,1,0:T(8,128)S(1)} %get-tuple-element.4) | data formatting | bytes 230400 | tf_op jit(solution)/shard_map/reshape | solution.py:447
  37.7 0.6 %copy.7 = f32[1,3600]{1,0:T(1,128)} copy(f32[1,3600]{1,0:T(1,128)S(1)} %get-tuple-element.9) | data formatting | bytes 28800

commit v5 on v4

--- a/solution.py
+++ b/solution.py
@@ -76,27 +76,30 @@
     return out
 
 
-def pack(D, ns, sides):
+def pack_side(D, side, at, mine):
+    lane = lanes((TILE, 128))
+    strip = jnp.zeros((TILE, 128), jnp.float32)
+    for item, first, depth in ITEMS:
+        whole = D[item, TOP : TOP + TILE]
+        strip = jnp.where(within(lane, first, depth), turn(whole, first - at * (TILE - depth)), strip)
+    for half, row in enumerate(HALVES):
+        side[half] = strip[row : row + 32]
+        side[half, 0:1] += mine
+
+
+def pack_ends(D, ns, mine):
     def both(item, north, south, count):
         return D[item, TOP + north : TOP + north + count] + turn(D[item, TOP + south : TOP + south + count], 64)
 
     for i in range(4):
-        ns[i // 2, 16 * (i % 2) : 16 * (i % 2) + 16] = both(4 + i, 0, 43, 16)
-        ns[3, 4 * i : 4 * i + 4] = both(i, 0, 56, 4)
-        ns[3, 16 + i : 17 + i] = both(4 + i, 16, 59, 1)
-    ns[2, 0:16] = both(ETA, 0, 44, 16)
-    ns[2, 16:32] = both(WET, 0, 44, 16)
-    ns[3, 20:32] = jnp.zeros((12, 128), jnp.float32)
-    lane = lanes((TILE, 128))
-    east = west = jnp.zeros((TILE, 128), jnp.float32)
-    for item, first, depth in ITEMS:
-        whole = D[item, TOP : TOP + TILE]
-        here = within(lane, first, depth)
-        east = jnp.where(here, turn(whole, first - (TILE - depth)), east)
-        west = jnp.where(here, turn(whole, first), west)
-    for half, row in enumerate(HALVES):
-        sides[0, half] = east[row : row + 32]
-        sides[1, half] = west[row : row + 32]
+        ns[i] = both(4 + i, 0, 43, 16)
+        ns[6, 4 * i : 4 * i + 4] = both(i, 0, 56, 4)
+        ns[7, i : i + 1] = both(4 + i, 16, 59, 1)
+    ns[4] = both(ETA, 0, 44, 16)
+    ns[5] = both(WET, 0, 44, 16)
+    ns[7, 4:16] = jnp.zeros((12, 128), jnp.float32)
+    for m in range(SUB):
+        ns[m, 0:1] += mine
 
 
 def take(table, index):
@@ -139,19 +142,19 @@
         D[item, TOP + south : TOP + south + count] = jnp.where(tile, rows, 0.0)
 
     for i in range(4):
-        put(4 + i, got[i // 2, 16 * (i % 2) : 16 * (i % 2) + 16], -17, 60)
-        put(4 + i, got[3, 16 + i : 17 + i], -1, 76)
-        put(i, got[3, 4 * i : 4 * i + 4], -4, 60)
-    put(ETA, got[2, 0:16], -16, 60)
-    put(WET, got[2, 16:32], -16, 60)
+        put(4 + i, got[i], -17, 60)
+        put(4 + i, got[7, i : i + 1], -1, 76)
+        put(i, got[6, 4 * i : 4 * i + 4], -4, 60)
+    put(ETA, got[4], -16, 60)
+    put(WET, got[5], -16, 60)
 
 
 def unpack_sides(D, got, eb, wb):
     for held, odd in ((eb, 0), (wb, 1)):
-        held[8:24] = got[2 + odd, 64:80]
+        held[8:24] = got[2 + odd, 32:48]
         for half, row in enumerate(HALVES):
-            held[TOP + row : TOP + row + 32] = got[2 * half + odd, 32:64]
-        held[84:100] = got[odd, 64:80]
+            held[TOP + row : TOP + row + 32] = got[2 * half + odd, 0:32]
+        held[84:100] = got[odd, 32:48]
 
     for item, first, depth in ITEMS:
         beyond = min(depth, 16)
@@ -163,36 +166,38 @@
         D[item, begin : begin + count] = D[item, begin : begin + count] + sides
 
 
-def clinic(D, N, wets, item, begin, count):
-    level = item % 2
-
+def clinic(D, N, wets, field, begin, count):
     def at(which, shift=0):
-        return D[which, begin + shift : begin + shift + count]
-
-    mid, north, south = at(item), at(item, -1), at(item, 1)
-    half_u = (0.5 * time_step) * at(4 + level)
-    half_v = (0.5 * time_step) * at(6 + level)
+        return D[2 * which : 2 * which + 2, begin + shift : begin + shift + count]
+
+    mid, north, south = at(field), at(field, -1), at(field, 1)
+    half_u = (0.5 * time_step) * at(2)
+    half_v = (0.5 * time_step) * at(3)
     right, left = turn(mid, -1), turn(mid, 1)
     pair = north + south
     cross = 2.0 * pair - 8.0 * mid
-    far = (at(item, -2) + at(item, 2)) + (turn(cross + right, -1) + turn(cross + left, 1))
+    far = (at(field, -2) + at(field, 2)) + (turn(cross + right, -1) + turn(cross + left, 1))
     rate = time_step * mixing
     new = (1.0 - 20.0 * rate) * mid + (8.0 * rate) * pair - rate * far
     new = new - half_u * (right - left) - half_v * (south - north)
-    if item // 2 == 2:
+    if field == 2:
         new = new + (2.0 * coriolis) * half_v
-    if item // 2 == 3:
+    if field == 3:
         new = new - (2.0 * coriolis) * half_u
-    N[item, begin : begin + count] = new * wets[begin : begin + count]
-    lane = lanes((2, 128))
+    N[2 * field : 2 * field + 2, begin : begin + count] = new * wets[begin : begin + count][None]
+
+
+def vertices(D, N, wets):
+    rate = time_step * mixing
+    lane = lanes((8, 2, 128))
     for row in (TOP - 1, TOP + TILE - 1):
-        swapped = jnp.concatenate([D[item, row + 1 : row + 2], D[item, row : row + 1]], 0)
+        swapped = jnp.concatenate([D[0:8, row + 1 : row + 2], D[0:8, row : row + 1]], 1)
         diagonal = jnp.where(
             (lane == 0) | (lane == TILE),
             turn(swapped, 1),
             jnp.where((lane == 127) | (lane == TILE - 1), turn(swapped, -1), 0.0),
         )
-        N[item, row : row + 2] += (2.0 * rate) * diagonal * wets[row : row + 2]
+        N[0:8, row : row + 2] += (2.0 * rate) * diagonal * wets[row : row + 2][None]
 
 
 def tropic(heights, norths, wet_at, eta, zonal, meridional, begin, count):
@@ -240,6 +245,8 @@
     own_in,
     side_in,
     lists,
+    out_ends,
+    got_ends,
     out,
     got,
     eb,
@@ -256,6 +263,13 @@
     turns = 1 - 2 * lax.rem(column, 2)
     close = [lax.rem(me + SUB + turns * k, SUB) for k in (2, 1, -1)]
 
+    loads = [
+        pltpu.make_async_copy(held, target, loaded.at[i])
+        for i, (held, target) in enumerate(((mask_in, mask), (surface_in, surface), (state_in, state), (near_in, near)))
+    ]
+    for load in loads:
+        load.start()
+
     barrier = pltpu.get_barrier_semaphore()
     for k in (4, 3, 5, 2, 6, 1, 7, 0):
         r = lax.rem(me + k, SUB)
@@ -263,12 +277,6 @@
         if k:
             pl.semaphore_signal(barrier, inc=1, device_id=(column, r), device_id_type=MESH)
 
-    loads = [
-        pltpu.make_async_copy(held, target, loaded.at[i])
-        for i, (held, target) in enumerate(((mask_in, mask), (surface_in, surface), (state_in, state), (near_in, near)))
-    ]
-    for load in loads:
-        load.start()
     D[...] = jnp.zeros_like(D)
 
     def put(item):
@@ -295,7 +303,6 @@
                 tails[8 + item : 9 + item],
                 put(item),
             )
-    pack(D, ns, sides)
     loads[3].wait()
     lane = lanes((1, 128))
     mine = jnp.zeros((1, 128), jnp.float32)
@@ -303,13 +310,6 @@
         listed = near[0, direction]
         slot = jnp.where(listed >= 0, listed - base * SUB, -1).astype(jnp.float32)
         mine = jnp.where(lane == TILE + direction, slot, mine)
-    for q in range(4):
-        ns[q, 0:1] += mine
-    mine = turn(mine, LISTED - TILE)
-    for half in range(2):
-        sides[0, half, 0:1] += mine
-        sides[1, half, 0:1] += mine
-    own_in[me] = ns[quarter]
 
     def send(source_ref, target, kind, device):
         pltpu.make_async_remote_copy(
@@ -324,13 +324,17 @@
     def wait(ref, semaphore):
         pltpu.make_async_copy(ref, ref, semaphore).wait()
 
+    pack_side(D, sides.at[0], 1, turn(mine, LISTED - TILE))
     pl.semaphore_wait(barrier, 15)
     for pair in pairs:
-        half = lax.rem(pair, 2)
-        send(sides.at[0, half], side_in.at[me], 1, (after, 2 * pair + 1))
-        send(sides.at[1, half], side_in.at[me], 1, (before, 2 * pair))
+        send(sides.at[0, lax.rem(pair, 2)], side_in.at[me], 1, (after, 2 * pair + 1))
+    pack_side(D, sides.at[1], 0, turn(mine, LISTED - TILE))
+    for pair in pairs:
+        send(sides.at[1, lax.rem(pair, 2)], side_in.at[me], 1, (before, 2 * pair))
+    pack_ends(D, ns, mine)
+    own_in[me] = ns[me]
     for r in others:
-        send(ns.at[lax.rem(r, 4)], own_in.at[me], 0, (column, r))
+        send(ns.at[r], own_in.at[me], 0, (column, r))
 
     N[...] = jnp.zeros_like(N)
     heights[...] = jnp.zeros_like(heights)
@@ -347,28 +351,27 @@
             target[slot, at + 8 * i : at + 8 * i + 8] = part
 
     def fill_sides(target, slot, r):
-        fill(target, slot, r, 1, side_in, 0, 32, 32)
-        fill(target, slot, r, 2, side_in, pl.multiple_of(16 * (quarter // 2), 16), 64, 16)
+        fill(target, slot, r, 1, side_in, 0, 0, 32)
+        fill(target, slot, r, 2, side_in, pl.multiple_of(16 * (quarter // 2), 16), 32, 16)
 
     seven, eight, three = pl.ds(0, SUB - 1), pl.ds(0, SUB), pl.ds(0, 3)
-    ends, flanks = pl.ds(0, 32), pl.ds(32, 48)
     wait(own_in.at[seven], came.at[0])
     wanted(own_in, me, lists)
-    for i, r in enumerate(close):
-        fill(out, i, r, 0, own_in, 0, 0, 32)
-        send(out.at[i, ends], got.at[quarter, ends], 2, (column, r))
-    fill(got, quarter, me, 0, own_in, 0, 0, 32)
+    for r in others:
+        fill(out_ends, r, r, 0, own_in, 0, 0, 16)
+        send(out_ends.at[r], got_ends.at[me], 2, (column, r))
+    fill(got_ends, me, me, 0, own_in, 0, 0, 16)
 
     wait(side_in.at[eight], came.at[1])
     corners(side_in, me, lists)
     for i, r in enumerate(close):
         fill_sides(out, i, r)
-        send(out.at[i, flanks], got.at[quarter, flanks], 3, (column, r))
+        send(out.at[i], got.at[quarter], 3, (column, r))
     fill_sides(got, quarter, me)
 
-    wait(got.at[three, ends], came.at[2])
-    unpack_ends(D, got)
-    wait(got.at[three, flanks], came.at[3])
+    wait(got_ends.at[seven], came.at[2])
+    unpack_ends(D, got_ends)
+    wait(got.at[three], came.at[3])
     unpack_sides(D, got, eb, wb)
     weights = (2.0 / 6.0, 4.0 / 6.0)
     fields, other = D, N
@@ -376,10 +379,11 @@
     for step in range(STEPS):
         begin, count = ((8, 96), (16, 80))[step]
         tracer = ((16, 72), (24, 64))[step]
-        for item in range(4):
-            clinic(fields, other, D.at[WET], item, *tracer)
-        for item in range(4, 8):
-            clinic(fields, other, D.at[WET], item, begin, count)
+        for field in (2, 3):
+            clinic(fields, other, D.at[WET], field, begin, count)
+        for field in (0, 1):
+            clinic(fields, other, D.at[WET], field, *tracer)
+        vertices(fields, other, D.at[WET])
         rows = slice(begin, begin + count)
         old_u = weights[0] * other[4, rows] + weights[1] * other[5, rows]
         old_v = weights[0] * other[6, rows] + weights[1] * other[7, rows]
@@ -401,8 +405,8 @@
 
     wait(own_in.at[seven], sent.at[0])
     wait(side_in.at[eight], sent.at[1])
-    wait(got.at[three, ends], sent.at[2])
-    wait(got.at[three, flanks], sent.at[3])
+    wait(got_ends.at[seven], sent.at[2])
+    wait(got.at[three], sent.at[3])
 
 
 def shards(columns, state, surface, land_mask, neighbours):
@@ -428,13 +432,15 @@
             f32(10, ROWS, 128),
             f32(ROWS, 128),
             f32(ROWS, 128),
-            f32(4, 32, 128),
+            f32(SUB, 16, 128),
             f32(2, 2, 32, 128),
-            f32(SUB, 32, 128),
+            f32(SUB, 16, 128),
             f32(SUB, 32, 128),
             f32(5, 8, 128),
-            f32(3, 80, 128),
-            f32(4, 80, 128),
+            f32(SUB, 16, 128),
+            f32(SUB, 16, 128),
+            f32(3, 48, 128),
+            f32(4, 48, 128),
             f32(ROWS, 128),
             f32(ROWS, 128),
             pltpu.SemaphoreType.DMA((4,)),

time: 38.5 us -> 38.2 us (level)
  no operation moved by 1% of the time
where the time goes in v5:
time: 38.2 us; the launch traced here: 38 us
  Pallas kernels  35.9 us (94%)
  local copies, waits for them, and re-layouts  1.52 us (4%)
  between operations  0.64 us (2%)
    pallas_call x1, Pallas kernels, shards(): pl.pallas_call(functools.partial(kernel, columns), out_shape=(jax.ShapeDt...  35.9 us
    reshape x1, local copies, waits for them, and re-layouts, shards(): return (new_state.reshape(state.shape), new_surface)  0.92 us

profile of v5, /device:TPU:16, one launch (start us, length us, event | category | flops | bytes accessed | tf_op | source)
XLA Modules:
  0.0 38.0 jit_solution(7428796751247976541)
XLA Ops:
  0.6 35.9 %shard_map.59 = (f32[8,60,60]{2,1,0:T(8,128)S(1)}, f32[1,3600]{1,0:T(1,128)S(1)}) custom-call(s32[1,4]{1,0:T(1,128)} %near_in.1, f32[1,4,2,3600]{3,2,1,0:T(2,128)} %state_in.1, f32[1,3600]{1,0:T(1,128)} %surface_in.1, s32[1,3600]{1,0:T(1,128)} %mask_in.1), custom_call_target="tpu_custom_call" | custom-call | tf_op jit(solution)/shard_map/pallas_call | solution.py:415
  36.5 0.9 %reshape.7 = f32[1,4,2,3600]{3,2,1,0:T(2,128)} reshape(f32[8,60,60]{2,1,0:T(8,128)S(1)} %get-tuple-element.4) | data formatting | bytes 230400 | tf_op jit(solution)/shard_map/reshape | solution.py:453
  37.4 0.6 %copy.7 = f32[1,3600]{1,0:T(1,128)} copy(f32[1,3600]{1,0:T(1,128)S(1)} %get-tuple-element.9) | data formatting | bytes 28800

commit v6 on v5

--- a/solution.py
+++ b/solution.py
@@ -211,10 +211,11 @@
         def c(shift):
             return norths[begin + shift : begin + shift + count]
 
-        new_u = zonal - (gravity_step * 0.5) * (turn(eta, -1) - turn(eta, 1))
-        new_v = meridional - (gravity_step * 0.5) * (a(1) - a(-1))
-        along = (c(1) - c(-1)) - (gravity_step * 0.5) * ((a(2) - eta) - (eta - a(-2)))
-        spread = (turn(new_u, -1) - turn(new_u, 1)) + along
+        pull = gravity_step * 0.5
+        new_u = zonal - pull * (turn(eta, -1) - turn(eta, 1))
+        new_v = meridional - pull * (a(1) - a(-1))
+        across = (turn(zonal, -1) - turn(zonal, 1)) + (c(1) - c(-1))
+        spread = across - pull * ((turn(eta, -2) + turn(eta, 2)) + (a(2) + a(-2)) - 4.0 * eta)
         wet = wet_at(begin, count)
         eta = (eta - (depth_step * 0.5) * spread) * wet
         zonal, meridional = new_u * wet, new_v * wet

time: 38.2 us -> 38.2 us (level)
  no operation moved by 1% of the time
where the time goes in v6:
time: 38.2 us; the launch traced here: 38 us
  Pallas kernels  35.9 us (94%)
  local copies, waits for them, and re-layouts  1.52 us (4%)
  between operations  0.64 us (2%)
    pallas_call x1, Pallas kernels, shards(): pl.pallas_call(functools.partial(kernel, columns), out_shape=(jax.ShapeDt...  35.9 us
    reshape x1, local copies, waits for them, and re-layouts, shards(): return (new_state.reshape(state.shape), new_surface)  0.92 us

profile of v6, /device:TPU:16, one launch (start us, length us, event | category | flops | bytes accessed | tf_op | source)
XLA Modules:
  0.0 38.0 jit_solution(9788152199557502470)
XLA Ops:
  0.6 35.9 %shard_map.59 = (f32[8,60,60]{2,1,0:T(8,128)S(1)}, f32[1,3600]{1,0:T(1,128)S(1)}) custom-call(s32[1,4]{1,0:T(1,128)} %near_in.1, f32[1,4,2,3600]{3,2,1,0:T(2,128)} %state_in.1, f32[1,3600]{1,0:T(1,128)} %surface_in.1, s32[1,3600]{1,0:T(1,128)} %mask_in.1), custom_call_target="tpu_custom_call" | custom-call | tf_op jit(solution)/shard_map/pallas_call | solution.py:416
  36.5 0.9 %reshape.7 = f32[1,4,2,3600]{3,2,1,0:T(2,128)} reshape(f32[8,60,60]{2,1,0:T(8,128)S(1)} %get-tuple-element.4) | data formatting | bytes 230400 | tf_op jit(solution)/shard_map/reshape | solution.py:454
  37.4 0.6 %copy.7 = f32[1,3600]{1,0:T(1,128)} copy(f32[1,3600]{1,0:T(1,128)S(1)} %get-tuple-element.9) | data formatting | bytes 28800
